TPU v7x, 128 devices: a whole 4x4x4 slice. The times are simulated.
128 devices in a mesh: blk: 8 (over y, x_lo), group: 16 (over z, x_hi, core).
Axes of the slice: x: 4 (x_hi: 2, x_lo: 2; x = x_hi * 2 + x_lo), y: 4, z: 4, core: 2. Of those that a mesh axis runs over, the one named last changes fastest.
Arguments:
- image_embeds: bfloat16 [16384, 768], P(('blk', 'group')), may hold values from -12 to 12
- text_embeds: bfloat16 [16384, 768], P(('blk', 'group')), may hold values from -12 to 12
- pair_weights: bfloat16 [16384], P(('blk', 'group')), may hold values from 0.19921875 to 5
- log_scale: float32 [1], replicated, may hold values from 2 to 2.5
- bias: float32 [1], replicated, may hold values from -15 to -11
Outputs:
- grad_image: float32 [16384, 768], P(('blk', 'group'))
- grad_text: float32 [16384, 768], P(('blk', 'group'))
- scalars: float32 [3], replicated
All inputs are finite; a program needn't handle non-finite values.
Results may differ from a plain program's by a relative error of at most 0.0013.
The roundings to bfloat16 on the way count: a program that leaves them out, or rounds other values in their place, can miss the bound.
Values may be sent and summed in bfloat16 or wider, within the bound.
No kernel may reach another device: no remote copies, remote signals or barrier semaphores. Data moves between devices by JAX's collectives and lax.ppermute only.
A program may use at most 64 MiB of HBM per device.

v0:
```python
import functools

import jax
import jax.numpy as jnp
from jax import lax
from jax.experimental import pallas as pl
from jax.experimental.pallas import tpu as pltpu
from jax.sharding import PartitionSpec as P

F32 = jnp.float32
BF16 = jnp.bfloat16
SEND = jnp.float16
SIDE = 4
AXES = ("blk", "group")
LANES = 128
TAIL = 16
CONTRACT_LAST = (((1,), (1,)), ((), ()))
CONTRACT_FIRST = (((0,), (0,)), ((), ()))


def place(x, y, z, core):
    return (y * 2 + x % 2) * 16 + (z * 2 + x // 2) * 2 + core


def pairs(move):
    found = []
    for x in range(SIDE):
        for y in range(SIDE):
            for z in range(SIDE):
                for core in range(2):
                    found.append((place(x, y, z, core), place(*move(x, y, z, core))))
    return found


def send(values, move):
    return lax.ppermute(values, AXES, pairs(move))


def pair_move(x, y, z, core):
    return (x ^ 1 if core == 0 else 3 - x, y, z, core)


def column_move(x, y, z, core):
    return (3 - x if core == 0 else x ^ 1, y, z, core)


def to_sibling(x, y, z, core):
    return (x, y, z, 1 - core)


def pair_step(step):
    return lambda x, y, z, core: (
        (x, y, (z + step) % SIDE, core) if core == 0 else (x, (y + step) % SIDE, z, core)
    )


def column_step(step):
    return lambda x, y, z, core: (
        (x, (y + step) % SIDE, z, core) if core == 0 else (x, y, (z + step) % SIDE, core)
    )


STEPS = (1, 3, 2)


def on_core():
    return lax.rem(lax.axis_index("group"), 2)


def row_norm_of(wide):
    return jnp.sqrt(jnp.sum(wide * wide, axis=1, keepdims=True) + 1e-06)


def column_of(weight_row, width):
    return jnp.transpose(jnp.broadcast_to(weight_row, (width, weight_row.shape[1])))


def prepare_kernel(img_ref, txt_ref, wgt_ref, pair_out, column_out):
    rows, width = img_ref.shape
    img = img_ref[...].astype(F32)
    img = (img / row_norm_of(img)).astype(BF16)
    txt = txt_ref[...].astype(F32)
    txt = (txt / row_norm_of(txt)).astype(BF16)
    here = pl.ds(0, rows)
    for out in (pair_out, column_out):
        out[pl.ds(rows, TAIL), :] = jnp.zeros((TAIL, width), BF16)
        out[pl.ds(rows, TAIL), pl.ds(0, rows)] = jnp.broadcast_to(wgt_ref[...], (TAIL, rows))

    @pl.when(on_core() == 0)
    def _():
        pair_out[here, :] = img
        column_out[here, :] = txt

    @pl.when(on_core() == 1)
    def _():
        pair_out[here, :] = txt
        column_out[here, :] = img


def join_kernel(*refs):
    pair_refs, column_refs, (pair_out, column_out) = refs[:2], refs[2:6], refs[6:]
    for blocks, out in ((pair_refs, pair_out), (column_refs, column_out)):
        rows = blocks[0].shape[0] - TAIL
        tail = pl.ds(len(blocks) * rows, TAIL)
        out[tail, :] = jnp.zeros((TAIL, out.shape[1]), BF16)
        for index, block in enumerate(blocks):
            out[pl.ds(index * rows, rows), :] = block[pl.ds(0, rows), :]
            out[tail, pl.ds(index * rows, rows)] = block[pl.ds(rows, TAIL), pl.ds(0, rows)]


def take_pairs(blocks, rows_out, wgt_out):
    span = blocks[0].shape[0] - TAIL
    for index, block in enumerate(blocks):
        rows_out[pl.ds(index * span, span), :] = block[pl.ds(0, span), :]
        if wgt_out is not None:
            weight = block[pl.ds(span, TAIL), :][0:1, :span].astype(F32)
            wgt_out[pl.ds(index * span, span), :] = column_of(weight, LANES)


def take_columns(blocks, rows_out, wgt_out):
    span = blocks[0].shape[0] - TAIL
    rows = span // SIDE
    for chip, block in enumerate(blocks):
        for index in range(SIDE):
            there = pl.ds((2 * index + chip) * rows, rows)
            rows_out[there, :] = block[pl.ds(index * rows, rows), :]
            if wgt_out is not None:
                weight = block[pl.ds(span, TAIL), :][0:1, index * rows : (index + 1) * rows]
                wgt_out[there, :] = column_of(weight.astype(F32), LANES)


def score_part(img_all, wgt_all, txt_all, scale, bias, own, coef_out, weighted_out, grad_out, sums_out):
    count, width = img_all.shape
    span = 256
    rows = 128
    zero = jnp.zeros((8, LANES), F32)
    loss, diff, score = zero, zero, zero
    same = lax.broadcasted_iota(jnp.int32, (rows, LANES), 0) == lax.broadcasted_iota(
        jnp.int32, (rows, LANES), 1
    )

    def fold(values):
        return jnp.sum(values.reshape(-1, 8, LANES), axis=0)

    for part in range(count // span):
        here = pl.ds(span * part, span)
        img = img_all[here, :]
        weight = wgt_all[here, :]
        weighted_out[here, :] = (img.astype(F32) * jnp.tile(weight, (1, width // LANES))).astype(
            BF16
        )
        scores = lax.dot_general(img, txt_all[...], CONTRACT_LAST, preferred_element_type=F32)
        for tile in range(scores.shape[1] // LANES):
            score_tile = scores[:, tile * LANES : (tile + 1) * LANES]
            grown = jnp.exp(score_tile * scale + bias)
            beyond = 1.0 + grown
            diffs = grown / beyond
            if own and part == 0 and tile == 0:
                diffs = jnp.concatenate(
                    [jnp.where(same, diffs[:rows] - 1.0, diffs[:rows]), diffs[rows:]], axis=0
                )
                matched = jnp.where(same, score_tile[:rows] * scale + bias, 0.0)
                loss = loss - fold(matched * weight[:rows])
            coef_out[here, pl.ds(tile * LANES, LANES)] = diffs.astype(BF16)
            if tile == 0:
                over, diff_row, score_row = grown, diffs, diffs * score_tile
            else:
                over = over * beyond + grown
                diff_row = diff_row + diffs
                score_row = score_row + diffs * score_tile
        loss = loss + fold(jnp.log1p(over) * weight)
        diff = diff + fold(diff_row * weight)
        score = score + fold(score_row * weight)
        grad_out[here, :] = jnp.dot(coef_out[here, :], txt_all[...], preferred_element_type=F32)
    sums_out[0] = loss
    sums_out[1] = score
    sums_out[2] = diff


def sibling_kernel(log_scale_ref, bias_ref, *refs):
    pair_refs, column_refs, pair_sib, column_sib = refs[:4], refs[4:6], refs[6:10], refs[10:12]
    grad_out, coef_out, weighted_out, txt_all, sums_out, img_all, wgt_all = refs[12:]

    @pl.when(on_core() == 0)
    def _():
        take_columns(column_refs, txt_all, None)
        take_columns(column_sib, img_all, wgt_all)

    @pl.when(on_core() == 1)
    def _():
        take_pairs(pair_refs, txt_all, None)
        take_pairs(pair_sib, img_all, wgt_all)

    scale = jnp.exp(jnp.full((1, LANES), log_scale_ref[0], F32))
    score_part(
        img_all, wgt_all, txt_all, scale, bias_ref[0], False, coef_out, weighted_out, grad_out, sums_out
    )


def own_kernel(log_scale_ref, bias_ref, *refs):
    pair_refs, column_refs, txt_all = refs[:4], refs[4:6], refs[6]
    grad_out, coef_out, weighted_out, sums_out, img_all, wgt_all = refs[7:]

    @pl.when(on_core() == 0)
    def _():
        take_pairs(pair_refs, img_all, wgt_all)

    @pl.when(on_core() == 1)
    def _():
        take_columns(column_refs, img_all, wgt_all)

    scale = jnp.exp(jnp.full((1, LANES), log_scale_ref[0], F32))
    score_part(
        img_all, wgt_all, txt_all, scale, bias_ref[0], True, coef_out, weighted_out, grad_out, sums_out
    )


def text_kernel(
    sib_sums,
    own_sums,
    wgt_ref,
    sib_coef,
    own_coef,
    sib_weighted,
    own_weighted,
    own_grad,
    moved_grad,
    pair_keep,
    pair_send,
    column_keep,
    column_send,
    sums_out,
):
    rows = wgt_ref.shape[1]
    span = 2 * rows

    def put_pair(index, values):
        if index == 0:
            pair_keep[...] = values
        else:
            pair_send[index - 1] = values

    def put_column(index, values):
        there = pl.ds(index * rows, rows)
        column_keep[there, :] = values[:rows]
        column_send[there, :] = values[rows:]

    for index in range(SIDE):
        here = pl.ds(span * index, span)
        img = own_grad[here, :] + moved_grad[here, :]
        txt = lax.dot_general(
            own_coef[:, here], own_weighted[...], CONTRACT_FIRST, preferred_element_type=F32
        ) + lax.dot_general(
            sib_coef[:, here], sib_weighted[...], CONTRACT_FIRST, preferred_element_type=F32
        )
        first = on_core() == 0
        put_pair(index, jnp.where(first, img, txt))
        put_column(index, jnp.where(first, txt, img))
    lane = lax.broadcasted_iota(jnp.int32, (1, LANES), 1)
    row = jnp.where(lane == 3, jnp.sum(wgt_ref[...].astype(F32), axis=1, keepdims=True), 0.0)
    for kind in range(3):
        part = jnp.sum(sib_sums[kind] + own_sums[kind], axis=0, keepdims=True)
        row = row + jnp.where(lane == kind, jnp.sum(part, axis=1, keepdims=True), 0.0)
    sums_out[...] = jnp.broadcast_to(row, sums_out.shape)


def finish_kernel(
    log_scale_ref, sums_ref, img_ref, txt_ref, wgt_ref, pair_sum, column_sum, img_out, txt_out, scalar_out
):
    rows, width = img_ref.shape
    scale = jnp.exp(jnp.full((1, LANES), log_scale_ref[0], F32))
    lane = lax.broadcasted_iota(jnp.int32, (1, LANES), 1)
    sums = jnp.sum(sums_ref[...], axis=0, keepdims=True)
    total = jnp.sum(jnp.where(lane == 3, sums, 0.0), axis=1, keepdims=True)
    pair_count = float(rows * 2 * SIDE**3)
    factor = jnp.tile(scale / total, (1, width // LANES))
    first = on_core() == 0

    def back(gradient, values):
        norm = row_norm_of(values)
        unit = values / norm
        inner = jnp.sum(unit * gradient, axis=1, keepdims=True)
        return pair_count * (gradient - unit * inner) / norm

    weight = jnp.tile(column_of(wgt_ref[...].astype(F32), LANES), (1, width // LANES))
    img_sum = jnp.where(first, pair_sum[...], column_sum[...])
    txt_sum = jnp.where(first, column_sum[...], pair_sum[...])
    img_out[...] = back(factor * weight * img_sum, img_ref[...].astype(F32))
    txt_out[...] = back(factor * txt_sum, txt_ref[...].astype(F32))
    ratio = sums / total
    scalar_out[...] = jnp.broadcast_to(jnp.where(lane == 1, scale * ratio, ratio), scalar_out.shape)


VMEM_MIB = 24
IN_VMEM = pl.BlockSpec(memory_space=pltpu.VMEM)
IN_SMEM = pl.BlockSpec(memory_space=pltpu.SMEM)


def call(kernel, shapes, scalars, arrays, flops, moved, scratch=(), limit=16):
    return pl.pallas_call(
        kernel,
        out_shape=[jax.ShapeDtypeStruct(shape, kind) for shape, kind in shapes],
        in_specs=[IN_SMEM] * len(scalars) + [IN_VMEM] * len(arrays),
        out_specs=[IN_VMEM] * len(shapes),
        scratch_shapes=[pltpu.VMEM(shape, kind) for shape, kind in scratch],
        compiler_params=pltpu.CompilerParams(vmem_limit_bytes=limit * 2**20),
        cost_estimate=pl.CostEstimate(flops=flops, bytes_accessed=moved, transcendentals=0),
    )(*scalars, *arrays)


def body(image_embeds, text_embeds, pair_weights, log_scale, bias):
    rows, width = image_embeds.shape
    span, tall = 2 * rows, 2 * SIDE * rows
    devices = 2 * SIDE**3
    weight_row = pair_weights.reshape(1, rows)
    pair_own, column_own = call(
        prepare_kernel,
        [((rows + TAIL, width), BF16)] * 2,
        [],
        [image_embeds, text_embeds, weight_row],
        2 * 8 * rows * width,
        8 * rows * width,
    )
    column_near = [column_own] + [send(column_own, column_step(step)) for step in STEPS]
    pair_near = [pair_own, send(pair_own, pair_move)]
    pair_all, column_all = call(
        join_kernel,
        [((span + TAIL, width), BF16), ((SIDE * rows + TAIL, width), BF16)],
        [],
        pair_near + column_near,
        1,
        24 * rows * width,
    )
    pairs_in = [pair_all] + [send(pair_all, pair_step(step)) for step in STEPS]
    columns_in = [column_all, send(column_all, column_move)]
    pairs_sib = [send(block, to_sibling) for block in pairs_in]
    columns_sib = [send(block, to_sibling) for block in columns_in]
    half = 4 * tall * tall * width
    square = (tall, tall)
    flat = (tall, width)
    keep = [((tall, width), BF16), ((tall, LANES), F32)]
    sums_shape = ((3, 8, LANES), F32)
    sib_grad, sib_coef, sib_weighted, txt_all, sib_sums = call(
        sibling_kernel,
        [(flat, F32), (square, BF16), (flat, BF16), (flat, BF16), sums_shape],
        [log_scale, bias],
        pairs_in + columns_in + pairs_sib + columns_sib,
        half,
        16 * tall * width,
        keep,
        VMEM_MIB,
    )
    moved_grad = send(sib_grad, to_sibling)
    own_grad, own_coef, own_weighted, own_sums = call(
        own_kernel,
        [(flat, F32), (square, BF16), (flat, BF16), sums_shape],
        [log_scale, bias],
        pairs_in + columns_in + [txt_all],
        half,
        16 * tall * width,
        keep,
        VMEM_MIB,
    )
    pair_keep, pair_send, column_keep, column_send, sums = call(
        text_kernel,
        [
            ((span, width), F32),
            ((SIDE - 1, span, width), F32),
            ((SIDE * rows, width), F32),
            ((SIDE * rows, width), F32),
            ((devices, LANES), F32),
        ],
        [],
        [sib_sums, own_sums, weight_row, sib_coef, own_coef, sib_weighted, own_weighted]
        + [own_grad, moved_grad],
        half,
        24 * tall * width,
        (),
        VMEM_MIB,
    )
    column_sum = column_keep + send(column_send.astype(SEND), column_move).astype(F32)
    pair_sum = pair_keep
    for index, step in enumerate(STEPS):
        pair_sum = pair_sum + send(pair_send[index].astype(SEND), pair_step(-step)).astype(F32)
    all_sums = lax.all_to_all(sums, AXES, 0, 0, tiled=True)
    pair_last = pair_sum[:rows] + send(pair_sum[rows:].astype(SEND), pair_move).astype(F32)
    column_last = column_sum[:rows]
    for index, step in enumerate(STEPS):
        block = column_sum[(index + 1) * rows : (index + 2) * rows]
        column_last = column_last + send(block.astype(SEND), column_step(-step)).astype(F32)
    grad_image, grad_text, scalars = call(
        finish_kernel,
        [((rows, width), F32), ((rows, width), F32), ((8, LANES), F32)],
        [log_scale],
        [all_sums, image_embeds, text_embeds, weight_row, pair_last, column_last],
        2 * 12 * rows * width,
        24 * rows * width,
    )
    return grad_image, grad_text, scalars[0, :3]


def solution(mesh):
    placed = (P(AXES, None), P(AXES, None), P(AXES), P(), P())
    return jax.shard_map(
        body,
        mesh=mesh,
        in_specs=placed,
        out_specs=(P(AXES, None), P(AXES, None), P()),
        check_vma=False,
    )
```

profile of v0, /device:TPU:1, one launch (start us, length us, event | category | flops | bytes accessed | tf_op | source)
XLA Modules:
  0.0 83.5 jit_solution(9208539707532311871)
XLA Ops:
  3.4 3.4 %collective-permute-start = (bf16[144,768]{1,0:T(8,128)(2,1)S(1)}, bf16[144,768]{1,0:T(8,128)(2,1)S(1)}, u32[]{:S(2)}, u32[]{:S(2)}) collective-permute-start(bf16[144,768]{1,0:T(8,128)(2,1)S(1)} %get-tuple-element.24.refs_0_), channel_id=1, source_target_pairs={{0,16},{1,19},{4,20},{5,23},{8,24},{9,27},{12,28},{13,31},{32,48},... | collective-permute-start | bytes 663560 | tf_op jit(solution)/shard_map/ppermute | solution.py:36
  6.8 3.6 %collective-permute-start.3 = (bf16[144,768]{1,0:T(8,128)(2,1)S(1)}, bf16[144,768]{1,0:T(8,128)(2,1)S(1)}, u32[]{:S(2)}, u32[]{:S(2)}) collective-permute-start(bf16[144,768]{1,0:T(8,128)(2,1)S(1)} %get-tuple-element.25.refs_2_), channel_id=1, source_target_pairs={{0,64},{1,9},{4,68},{5,13},{8,72},{9,1},{12,76},{13,5},{32,96},{33... | collective-permute-start | bytes 663560 | tf_op jit(solution)/shard_map/ppermute | solution.py:36
  10.8 1.0 %collective-permute-start.1 = (bf16[144,768]{1,0:T(8,128)(2,1)S(1)}, bf16[144,768]{1,0:T(8,128)(2,1)S(1)}, u32[]{:S(2)}, u32[]{:S(2)}) collective-permute-start(bf16[144,768]{1,0:T(8,128)(2,1)S(1)} %get-tuple-element.25.refs_2_), channel_id=1, source_target_pairs={{0,32},{1,5},{4,36},{5,9},{8,40},{9,13},{12,44},{13,1},{32,64},{33... | collective-permute-start | bytes 663560 | tf_op jit(solution)/shard_map/ppermute | solution.py:36
  11.8 1.9 %collective-permute-done.3.refs_5_ = bf16[144,768]{1,0:T(8,128)(2,1)S(1)} collective-permute-done((bf16[144,768]{1,0:T(8,128)(2,1)S(1)}, bf16[144,768]{1,0:T(8,128)(2,1)S(1)}, u32[]{:S(2)}, u32[]{:S(2)}) %collective-permute-start.3) | collective-permute-done | bytes 221216 | tf_op jit(solution)/shard_map/ppermute | solution.py:36
  13.7 3.4 %collective-permute-done.2.refs_4_ = bf16[144,768]{1,0:T(8,128)(2,1)S(1)} collective-permute-done((bf16[144,768]{1,0:T(8,128)(2,1)S(1)}, bf16[144,768]{1,0:T(8,128)(2,1)S(1)}, u32[]{:S(2)}, u32[]{:S(2)}) %collective-permute-start.2) | collective-permute-done | bytes 221216 | tf_op jit(solution)/shard_map/ppermute | solution.py:36
  17.3 2.8 %collective-permute-start.8 = (bf16[272,768]{1,0:T(8,128)(2,1)S(1)}, bf16[272,768]{1,0:T(8,128)(2,1)S(1)}, u32[]{:S(2)}, u32[]{:S(2)}) collective-permute-start(bf16[272,768]{1,0:T(8,128)(2,1)S(1)} %get-tuple-element.26.refs_0_), channel_id=1, source_target_pairs={{0,1},{1,0},{4,5},{5,4},{8,9},{9,8},{12,13},{13,12},{32,33},{33,32... | collective-permute-start | bytes 1253384 | tf_op jit(solution)/shard_map/ppermute | solution.py:36
  20.1 1.3 %collective-permute-start.6 = (bf16[272,768]{1,0:T(8,128)(2,1)S(1)}, bf16[272,768]{1,0:T(8,128)(2,1)S(1)}, u32[]{:S(2)}, u32[]{:S(2)}) collective-permute-start(bf16[272,768]{1,0:T(8,128)(2,1)S(1)} %get-tuple-element.26.refs_0_), channel_id=1, source_target_pairs={{0,8},{1,65},{4,12},{5,69},{8,0},{9,73},{12,4},{13,77},{32,40},{33... | collective-permute-start | bytes 1253384 | tf_op jit(solution)/shard_map/ppermute | solution.py:36
  22.9 3.1 %collective-permute-start.12 = (bf16[528,768]{1,0:T(8,128)(2,1)S(1)}, bf16[528,768]{1,0:T(8,128)(2,1)S(1)}, u32[]{:S(2)}, u32[]{:S(2)}) collective-permute-start(bf16[528,768]{1,0:T(8,128)(2,1)S(1)} %get-tuple-element.27.refs_4_), channel_id=1, source_target_pairs={{0,1},{1,0},{4,5},{5,4},{8,9},{9,8},{12,13},{13,12},{32,33},{33,32... | collective-permute-start | bytes 2433032 | tf_op jit(solution)/shard_map/ppermute | solution.py:36
  26.0 2.7 %collective-permute-done.7.refs_5_ = bf16[528,768]{1,0:T(8,128)(2,1)S(1)} collective-permute-done((bf16[528,768]{1,0:T(8,128)(2,1)S(1)}, bf16[528,768]{1,0:T(8,128)(2,1)S(1)}, u32[]{:S(2)}, u32[]{:S(2)}) %collective-permute-start.7) | collective-permute-done | bytes 811040 | tf_op jit(solution)/shard_map/ppermute | solution.py:36
  28.7 2.8 %collective-permute-start.13 = (bf16[528,768]{1,0:T(8,128)(2,1)S(1)}, bf16[528,768]{1,0:T(8,128)(2,1)S(1)}, u32[]{:S(2)}, u32[]{:S(2)}) collective-permute-start(bf16[528,768]{1,0:T(8,128)(2,1)S(1)} %collective-permute-done.7.refs_5_), channel_id=1, source_target_pairs={{0,1},{1,0},{4,5},{5,4},{8,9},{9,8},{12,13},{13,12},{32,33},{33,32... | collective-permute-start | bytes 2433032 | tf_op jit(solution)/shard_map/ppermute | solution.py:36
  32.1 3.5 %collective-permute-start.10 = (bf16[272,768]{1,0:T(8,128)(2,1)S(1)}, bf16[272,768]{1,0:T(8,128)(2,1)S(1)}, u32[]{:S(2)}, u32[]{:S(2)}) collective-permute-start(bf16[272,768]{1,0:T(8,128)(2,1)S(1)} %collective-permute-done.5.refs_2_), channel_id=1, source_target_pairs={{0,1},{1,0},{4,5},{5,4},{8,9},{9,8},{12,13},{13,12},{32,33},{33,32... | collective-permute-start | bytes 1253384 | tf_op jit(solution)/shard_map/ppermute | solution.py:36
  37.5 4.9 %shard_map.78 = (f32[1024,768]{1,0:T(8,128)S(1)}, bf16[1024,1024]{1,0:T(8,128)(2,1)S(1)}, bf16[1024,768]{1,0:T(8,128)(2,1)S(1)}, bf16[1024,768]{1,0:T(8,128)(2,1)S(1)}, f32[3,8,128]{2,1,0:T(8,128)S(1)}) custom-call(f32[1]{0:T(128)S(6)} %copy.9.log_scale_ref, f32[1]{0:T(128)S(6)} %copy.10.bias_ref, bf16[272,768]{1,0:T(8,128)(2,1)S(1)} %get-tuple-element.26.refs_0_, ...), custom_call_target="tpu_custom_call" | custom-call | flops 3221225472 | bytes 12582912 | tf_op jit(solution)/shard_map/pallas_call | solution.py:300
  42.8 4.9 %shard_map.79 = (f32[1024,768]{1,0:T(8,128)S(1)}, bf16[1024,1024]{1,0:T(8,128)(2,1)S(1)}, bf16[1024,768]{1,0:T(8,128)(2,1)S(1)}, f32[3,8,128]{2,1,0:T(8,128)S(1)}) custom-call(f32[1]{0:T(128)S(6)} %copy.9.log_scale_ref, f32[1]{0:T(128)S(6)} %copy.10.bias_ref, bf16[272,768]{1,0:T(8,128)(2,1)S(1)} %get-tuple-element.26.refs_0_, ...), custom_call_target="tpu_custom_call" | custom-call | flops 3221225472 | bytes 12582912 | tf_op jit(solution)/shard_map/pallas_call | solution.py:300
  48.1 4.1 %shard_map.80 = (f32[256,768]{1,0:T(8,128)S(1)}, f32[3,256,768]{2,1,0:T(8,128)S(1)}, f32[512,768]{1,0:T(8,128)S(1)}, f32[512,768]{1,0:T(8,128)S(1)}, f32[128,128]{1,0:T(8,128)}) custom-call(f32[3,8,128]{2,1,0:T(8,128)S(1)} %get-tuple-element.28.sib_sums, f32[3,8,128]{2,1,0:T(8,128)S(1)} %get-tuple-element.30.own_sums, bf16[1,128]{1,0:T(2,128)(2,1)S(1)} %bitcast.15, ...), custom_call_target="tpu_custom_call" | custom-call | flops 3221225472 | bytes 18874368 | tf_op jit(solution)/shard_map/pallas_call | solution.py:300
  52.4 1.1 %slice_bitcast_fusion.2 = (f16[256,768]{1,0:T(8,128)(2,1)}, f16[256,768]{1,0:T(8,128)(2,1)}, f16[256,768]{1,0:T(8,128)(2,1)}) fusion(f16[3,256,768]{2,1,0:T(8,128)(2,1)S(1)} %convert.13), kind=kLoop, calls=%fused_computation.9 | loop fusion | bytes 2359296 | tf_op jit(solution)/shard_map/convert_element_type | solution.py:384
  53.5 1.2 %collective-permute-start.15 = (f16[256,768]{1,0:T(8,128)(2,1)}, f16[256,768]{1,0:T(8,128)(2,1)}, u32[]{:S(2)}, u32[]{:S(2)}) collective-permute-start(f16[256,768]{1,0:T(8,128)(2,1)} %get-tuple-element.47), channel_id=1, source_target_pairs={{0,12},{1,97},{4,0},{5,101},{8,4},{9,105},{12,8},{13,109},{32,44},... | collective-permute-start | bytes 1179656 | tf_op jit(solution)/shard_map/ppermute | solution.py:36
  57.0 8.6 %all-to-all-start = ((f32[128,1,128]{2,1,0:T(1,128)}), f32[128,1,128]{2,1,0:T(1,128)S(1)}, u32[]{:S(2)}, u32[]{:S(2)}) async-start(f32[128,1,128]{2,1,0:T(1,128)} %bitcast.2), calls=%async_computation | async-start | bytes 131072 | tf_op jit(solution)/shard_map/all_to_all | solution.py:385
  65.6 2.0 %collective-permute-done.16 = f16[256,768]{1,0:T(8,128)(2,1)} collective-permute-done((f16[256,768]{1,0:T(8,128)(2,1)}, f16[256,768]{1,0:T(8,128)(2,1)}, u32[]{:S(2)}, u32[]{:S(2)}) %collective-permute-start.16) | collective-permute-done | bytes 393248 | tf_op jit(solution)/shard_map/ppermute | solution.py:36
  67.6 1.4 %convert_add_fusion.1 = f32[256,768]{1,0:T(8,128)S(1)} fusion(f16[256,768]{1,0:T(8,128)(2,1)} %collective-permute-done.17, f16[256,768]{1,0:T(8,128)(2,1)} %collective-permute-done.16, f32[256,768]{1,0:T(8,128)S(1)} %get-tuple-element.38, f16[256,768]{1,0:T(8,128)(2,1)} %collective-permute-done.15), kind=kLoop, calls=%fused_computation.1 | loop fusion | flops 1179648 | bytes 2752512 | tf_op jit(solution)/shard_map/add | solution.py:384
  70.4 2.9 %collective-permute-start.20 = (f16[128,768]{1,0:T(8,128)(2,1)S(1)}, f16[128,768]{1,0:T(8,128)(2,1)S(1)}, u32[]{:S(2)}, u32[]{:S(2)}) collective-permute-start(f16[128,768]{1,0:T(8,128)(2,1)S(1)} %get-tuple-element.50), channel_id=1, source_target_pairs={{0,96},{1,13},{4,100},{5,1},{8,104},{9,5},{12,108},{13,9},{32,0},{... | collective-permute-start | bytes 589832 | tf_op jit(solution)/shard_map/ppermute | solution.py:36
  75.2 2.9 %collective-permute-done.20 = f16[128,768]{1,0:T(8,128)(2,1)S(1)} collective-permute-done((f16[128,768]{1,0:T(8,128)(2,1)S(1)}, f16[128,768]{1,0:T(8,128)(2,1)S(1)}, u32[]{:S(2)}, u32[]{:S(2)}) %collective-permute-start.20) | collective-permute-done | bytes 196640 | tf_op jit(solution)/shard_map/ppermute | solution.py:36
  78.1 1.6 %collective-permute-done.22 = f16[128,768]{1,0:T(8,128)(2,1)S(1)} collective-permute-done((f16[128,768]{1,0:T(8,128)(2,1)S(1)}, f16[128,768]{1,0:T(8,128)(2,1)S(1)}, u32[]{:S(2)}, u32[]{:S(2)}) %collective-permute-start.22) | collective-permute-done | bytes 196640 | tf_op jit(solution)/shard_map/ppermute | solution.py:36
  79.7 1.9 %collective-permute-done.21 = f16[128,768]{1,0:T(8,128)(2,1)S(1)} collective-permute-done((f16[128,768]{1,0:T(8,128)(2,1)S(1)}, f16[128,768]{1,0:T(8,128)(2,1)S(1)}, u32[]{:S(2)}, u32[]{:S(2)}) %collective-permute-start.21) | collective-permute-done | bytes 196640 | tf_op jit(solution)/shard_map/ppermute | solution.py:36
  81.7 1.3 %shard_map.81 = (f32[128,768]{1,0:T(8,128)}, f32[128,768]{1,0:T(8,128)}, f32[8,128]{1,0:T(8,128)S(1)}) custom-call(f32[1]{0:T(128)S(6)} %copy.9.log_scale_ref, f32[128,128]{1,0:T(8,128)S(1)} %bitcast.13, bf16[128,768]{1,0:T(8,128)(2,1)S(1)} %copy-done.1, bf16[128,768]{1,0:T(8,128)(2,1)S(1)} %copy-done.3, bf16[1,128]{1,0:T(2,128)(2,1)S(1)} %bitcast.16, ...), custom_call_target="tpu_custom_call" | custom-call | flops 2359296 | bytes 2359296 | tf_op jit(solution)/shard_map/pallas_call | solution.py:300
  (52 shorter events, 13.2 us)
Async XLA Ops:
  3.4 8.5 %collective-permute-start = (bf16[144,768]{1,0:T(8,128)(2,1)S(1)}, bf16[144,768]{1,0:T(8,128)(2,1)S(1)}, u32[]{:S(2)}, u32[]{:S(2)}) collective-permute-start(bf16[144,768]{1,0:T(8,128)(2,1)S(1)} %get-tuple-element.24.refs_0_), channel_id=1, source_target_pairs={{0,16},{1,19},{4,20},{5,23},{8,24},{9,27},{12,28},{13,31},{32,48},... | collective-permute-start | bytes 663560 | tf_op jit(solution)/shard_map/ppermute | solution.py:36
  6.8 6.9 %collective-permute-start.3 = (bf16[144,768]{1,0:T(8,128)(2,1)S(1)}, bf16[144,768]{1,0:T(8,128)(2,1)S(1)}, u32[]{:S(2)}, u32[]{:S(2)}) collective-permute-start(bf16[144,768]{1,0:T(8,128)(2,1)S(1)} %get-tuple-element.25.refs_2_), channel_id=1, source_target_pairs={{0,64},{1,9},{4,68},{5,13},{8,72},{9,1},{12,76},{13,5},{32,96},{33... | collective-permute-start | bytes 663560 | tf_op jit(solution)/shard_map/ppermute | solution.py:36
  10.4 6.8 %collective-permute-start.2 = (bf16[144,768]{1,0:T(8,128)(2,1)S(1)}, bf16[144,768]{1,0:T(8,128)(2,1)S(1)}, u32[]{:S(2)}, u32[]{:S(2)}) collective-permute-start(bf16[144,768]{1,0:T(8,128)(2,1)S(1)} %get-tuple-element.25.refs_2_), channel_id=1, source_target_pairs={{0,96},{1,13},{4,100},{5,1},{8,104},{9,5},{12,108},{13,9},{32,0},{... | collective-permute-start | bytes 663560 | tf_op jit(solution)/shard_map/ppermute | solution.py:36
  10.8 6.3 %collective-permute-start.1 = (bf16[144,768]{1,0:T(8,128)(2,1)S(1)}, bf16[144,768]{1,0:T(8,128)(2,1)S(1)}, u32[]{:S(2)}, u32[]{:S(2)}) collective-permute-start(bf16[144,768]{1,0:T(8,128)(2,1)S(1)} %get-tuple-element.25.refs_2_), channel_id=1, source_target_pairs={{0,32},{1,5},{4,36},{5,9},{8,40},{9,13},{12,44},{13,1},{32,64},{33... | collective-permute-start | bytes 663560 | tf_op jit(solution)/shard_map/ppermute | solution.py:36
  17.2 11.5 %collective-permute-start.7 = (bf16[528,768]{1,0:T(8,128)(2,1)S(1)}, bf16[528,768]{1,0:T(8,128)(2,1)S(1)}, u32[]{:S(2)}, u32[]{:S(2)}) collective-permute-start(bf16[528,768]{1,0:T(8,128)(2,1)S(1)} %get-tuple-element.27.refs_4_), channel_id=1, source_target_pairs={{0,18},{1,17},{4,22},{5,21},{8,26},{9,25},{12,30},{13,29},{32,50},... | collective-permute-start | bytes 2433032 | tf_op jit(solution)/shard_map/ppermute | solution.py:36
  17.3 5.6 %collective-permute-start.8 = (bf16[272,768]{1,0:T(8,128)(2,1)S(1)}, bf16[272,768]{1,0:T(8,128)(2,1)S(1)}, u32[]{:S(2)}, u32[]{:S(2)}) collective-permute-start(bf16[272,768]{1,0:T(8,128)(2,1)S(1)} %get-tuple-element.26.refs_0_), channel_id=1, source_target_pairs={{0,1},{1,0},{4,5},{5,4},{8,9},{9,8},{12,13},{13,12},{32,33},{33,32... | collective-permute-start | bytes 1253384 | tf_op jit(solution)/shard_map/ppermute | solution.py:36
  20.1 11.4 %collective-permute-start.6 = (bf16[272,768]{1,0:T(8,128)(2,1)S(1)}, bf16[272,768]{1,0:T(8,128)(2,1)S(1)}, u32[]{:S(2)}, u32[]{:S(2)}) collective-permute-start(bf16[272,768]{1,0:T(8,128)(2,1)S(1)} %get-tuple-element.26.refs_0_), channel_id=1, source_target_pairs={{0,8},{1,65},{4,12},{5,69},{8,0},{9,73},{12,4},{13,77},{32,40},{33... | collective-permute-start | bytes 1253384 | tf_op jit(solution)/shard_map/ppermute | solution.py:36
  21.4 10.6 %collective-permute-start.5 = (bf16[272,768]{1,0:T(8,128)(2,1)S(1)}, bf16[272,768]{1,0:T(8,128)(2,1)S(1)}, u32[]{:S(2)}, u32[]{:S(2)}) collective-permute-start(bf16[272,768]{1,0:T(8,128)(2,1)S(1)} %get-tuple-element.26.refs_0_), channel_id=1, source_target_pairs={{0,12},{1,97},{4,0},{5,101},{8,4},{9,105},{12,8},{13,109},{32,44},... | collective-permute-start | bytes 1253384 | tf_op jit(solution)/shard_map/ppermute | solution.py:36
  22.3 13.2 %collective-permute-start.4 = (bf16[272,768]{1,0:T(8,128)(2,1)S(1)}, bf16[272,768]{1,0:T(8,128)(2,1)S(1)}, u32[]{:S(2)}, u32[]{:S(2)}) collective-permute-start(bf16[272,768]{1,0:T(8,128)(2,1)S(1)} %get-tuple-element.26.refs_0_), channel_id=1, source_target_pairs={{0,4},{1,33},{4,8},{5,37},{8,12},{9,41},{12,0},{13,45},{32,36},{33... | collective-permute-start | bytes 1253384 | tf_op jit(solution)/shard_map/ppermute | solution.py:36
  22.9 13.9 %collective-permute-start.12 = (bf16[528,768]{1,0:T(8,128)(2,1)S(1)}, bf16[528,768]{1,0:T(8,128)(2,1)S(1)}, u32[]{:S(2)}, u32[]{:S(2)}) collective-permute-start(bf16[528,768]{1,0:T(8,128)(2,1)S(1)} %get-tuple-element.27.refs_4_), channel_id=1, source_target_pairs={{0,1},{1,0},{4,5},{5,4},{8,9},{9,8},{12,13},{13,12},{32,33},{33,32... | collective-permute-start | bytes 2433032 | tf_op jit(solution)/shard_map/ppermute | solution.py:36
  28.7 8.8 %collective-permute-start.13 = (bf16[528,768]{1,0:T(8,128)(2,1)S(1)}, bf16[528,768]{1,0:T(8,128)(2,1)S(1)}, u32[]{:S(2)}, u32[]{:S(2)}) collective-permute-start(bf16[528,768]{1,0:T(8,128)(2,1)S(1)} %collective-permute-done.7.refs_5_), channel_id=1, source_target_pairs={{0,1},{1,0},{4,5},{5,4},{8,9},{9,8},{12,13},{13,12},{32,33},{33,32... | collective-permute-start | bytes 2433032 | tf_op jit(solution)/shard_map/ppermute | solution.py:36
  31.5 5.4 %collective-permute-start.11 = (bf16[272,768]{1,0:T(8,128)(2,1)S(1)}, bf16[272,768]{1,0:T(8,128)(2,1)S(1)}, u32[]{:S(2)}, u32[]{:S(2)}) collective-permute-start(bf16[272,768]{1,0:T(8,128)(2,1)S(1)} %collective-permute-done.6.refs_3_), channel_id=1, source_target_pairs={{0,1},{1,0},{4,5},{5,4},{8,9},{9,8},{12,13},{13,12},{32,33},{33,32... | collective-permute-start | bytes 1253384 | tf_op jit(solution)/shard_map/ppermute | solution.py:36
  32.1 4.8 %collective-permute-start.10 = (bf16[272,768]{1,0:T(8,128)(2,1)S(1)}, bf16[272,768]{1,0:T(8,128)(2,1)S(1)}, u32[]{:S(2)}, u32[]{:S(2)}) collective-permute-start(bf16[272,768]{1,0:T(8,128)(2,1)S(1)} %collective-permute-done.5.refs_2_), channel_id=1, source_target_pairs={{0,1},{1,0},{4,5},{5,4},{8,9},{9,8},{12,13},{13,12},{32,33},{33,32... | collective-permute-start | bytes 1253384 | tf_op jit(solution)/shard_map/ppermute | solution.py:36
  35.5 2.0 %collective-permute-start.9 = (bf16[272,768]{1,0:T(8,128)(2,1)S(1)}, bf16[272,768]{1,0:T(8,128)(2,1)S(1)}, u32[]{:S(2)}, u32[]{:S(2)}) collective-permute-start(bf16[272,768]{1,0:T(8,128)(2,1)S(1)} %collective-permute-done.4.refs_1_), channel_id=1, source_target_pairs={{0,1},{1,0},{4,5},{5,4},{8,9},{9,8},{12,13},{13,12},{32,33},{33,32... | collective-permute-start | bytes 1253384 | tf_op jit(solution)/shard_map/ppermute | solution.py:36
  42.4 5.7 %collective-permute-start.14 = (f32[1024,768]{1,0:T(8,128)S(1)}, f32[1024,768]{1,0:T(8,128)S(1)}, u32[]{:S(2)}, u32[]{:S(2)}) collective-permute-start(f32[1024,768]{1,0:T(8,128)S(1)} %get-tuple-element.36), channel_id=1, source_target_pairs={{0,1},{1,0},{4,5},{5,4},{8,9},{9,8},{12,13},{13,12},{32,33},{33,32... | collective-permute-start | bytes 9437192 | tf_op jit(solution)/shard_map/ppermute | solution.py:36
  53.5 12.1 %collective-permute-start.15 = (f16[256,768]{1,0:T(8,128)(2,1)}, f16[256,768]{1,0:T(8,128)(2,1)}, u32[]{:S(2)}, u32[]{:S(2)}) collective-permute-start(f16[256,768]{1,0:T(8,128)(2,1)} %get-tuple-element.47), channel_id=1, source_target_pairs={{0,12},{1,97},{4,0},{5,101},{8,4},{9,105},{12,8},{13,109},{32,44},... | collective-permute-start | bytes 1179656 | tf_op jit(solution)/shard_map/ppermute | solution.py:36
  54.7 11.0 %collective-permute-start.17 = (f16[256,768]{1,0:T(8,128)(2,1)}, f16[256,768]{1,0:T(8,128)(2,1)}, u32[]{:S(2)}, u32[]{:S(2)}) collective-permute-start(f16[256,768]{1,0:T(8,128)(2,1)} %get-tuple-element.48), channel_id=1, source_target_pairs={{0,8},{1,65},{4,12},{5,69},{8,0},{9,73},{12,4},{13,77},{32,40},{33... | collective-permute-start | bytes 1179656 | tf_op jit(solution)/shard_map/ppermute | solution.py:36
  55.1 12.5 %collective-permute-start.16 = (f16[256,768]{1,0:T(8,128)(2,1)}, f16[256,768]{1,0:T(8,128)(2,1)}, u32[]{:S(2)}, u32[]{:S(2)}) collective-permute-start(f16[256,768]{1,0:T(8,128)(2,1)} %get-tuple-element.49), channel_id=1, source_target_pairs={{0,4},{1,33},{4,8},{5,37},{8,12},{9,41},{12,0},{13,45},{32,36},{33... | collective-permute-start | bytes 1179656 | tf_op jit(solution)/shard_map/ppermute | solution.py:36
  56.7 13.3 %collective-permute-start.19 = (f16[512,768]{1,0:T(8,128)(2,1)}, f16[512,768]{1,0:T(8,128)(2,1)S(1)}, u32[]{:S(2)}, u32[]{:S(2)}) collective-permute-start(f16[512,768]{1,0:T(8,128)(2,1)} %convert_element_type.50), channel_id=1, source_target_pairs={{0,18},{1,17},{4,22},{5,21},{8,26},{9,25},{12,30},{13,29},{32,50},... | collective-permute-start | bytes 2359304 | tf_op jit(solution)/shard_map/ppermute | solution.py:36
  57.0 24.7 %all-to-all-start = ((f32[128,1,128]{2,1,0:T(1,128)}), f32[128,1,128]{2,1,0:T(1,128)S(1)}, u32[]{:S(2)}, u32[]{:S(2)}) async-start(f32[128,1,128]{2,1,0:T(1,128)} %bitcast.2), calls=%async_computation | async-start | bytes 131072 | tf_op jit(solution)/shard_map/all_to_all | solution.py:385
  69.0 6.1 %collective-permute-start.18 = (f16[128,768]{1,0:T(8,128)(2,1)S(1)}, f16[128,768]{1,0:T(8,128)(2,1)S(1)}, u32[]{:S(2)}, u32[]{:S(2)}) collective-permute-start(f16[128,768]{1,0:T(8,128)(2,1)S(1)} %slice_convert_fusion), channel_id=1, source_target_pairs={{0,16},{1,19},{4,20},{5,23},{8,24},{9,27},{12,28},{13,31},{32,48},... | collective-permute-start | bytes 589832 | tf_op jit(solution)/shard_map/ppermute | solution.py:36
  70.4 7.7 %collective-permute-start.20 = (f16[128,768]{1,0:T(8,128)(2,1)S(1)}, f16[128,768]{1,0:T(8,128)(2,1)S(1)}, u32[]{:S(2)}, u32[]{:S(2)}) collective-permute-start(f16[128,768]{1,0:T(8,128)(2,1)S(1)} %get-tuple-element.50), channel_id=1, source_target_pairs={{0,96},{1,13},{4,100},{5,1},{8,104},{9,5},{12,108},{13,9},{32,0},{... | collective-permute-start | bytes 589832 | tf_op jit(solution)/shard_map/ppermute | solution.py:36
  73.3 6.4 %collective-permute-start.22 = (f16[128,768]{1,0:T(8,128)(2,1)S(1)}, f16[128,768]{1,0:T(8,128)(2,1)S(1)}, u32[]{:S(2)}, u32[]{:S(2)}) collective-permute-start(f16[128,768]{1,0:T(8,128)(2,1)S(1)} %get-tuple-element.51), channel_id=1, source_target_pairs={{0,64},{1,9},{4,68},{5,13},{8,72},{9,1},{12,76},{13,5},{32,96},{33... | collective-permute-start | bytes 589832 | tf_op jit(solution)/shard_map/ppermute | solution.py:36
  73.4 8.1 %collective-permute-start.21 = (f16[128,768]{1,0:T(8,128)(2,1)S(1)}, f16[128,768]{1,0:T(8,128)(2,1)S(1)}, u32[]{:S(2)}, u32[]{:S(2)}) collective-permute-start(f16[128,768]{1,0:T(8,128)(2,1)S(1)} %get-tuple-element.52), channel_id=1, source_target_pairs={{0,32},{1,5},{4,36},{5,9},{8,40},{9,13},{12,44},{13,1},{32,64},{33... | collective-permute-start | bytes 589832 | tf_op jit(solution)/shard_map/ppermute | solution.py:36
  (6 other events, 30.7 us)
where the time goes:
time: 85 us; the launch traced here: 83.5 us
  starting transfers between devices  39.8 us (47%)
  waiting for transfers between devices  18.9 us (22%)
  Pallas kernels  15.5 us (18%)
  local copies, waits for them, and re-layouts  4.22 us (5%)
  other arithmetic  2.94 us (3%)
  between operations  2.11 us (2%)
    ppermute x23, starting transfers between devices, send(): return lax.ppermute(values, AXES, pairs(move))  31.2 us
    ppermute x23, waiting for transfers between devices, send(): return lax.ppermute(values, AXES, pairs(move))  18.9 us
    pallas_call x6, Pallas kernels, call(): pl.pallas_call(kernel, out_shape=[jax.ShapeDtypeStruct(shape, kind) for s...  15.5 us
    all_to_all x1, starting transfers between devices, body(): all_sums = lax.all_to_all(sums, AXES, 0, 0, tiled=True)  8.62 us
    unnamed x12, local copies, waits for them, and re-layouts  2.52 us
  transfers between devices with their start and end apart: 24, of which 12 were waited for; matrix products, arithmetic and copies ran while one was open for 3% of the time, Pallas kernels for 6%

commit v1 on v0

v1 whole, which is shorter than its diff:
```python
import functools

import jax
import jax.numpy as jnp
from jax import lax
from jax.experimental import pallas as pl
from jax.experimental.pallas import tpu as pltpu
from jax.sharding import PartitionSpec as P

F32 = jnp.float32
BF16 = jnp.bfloat16
SEND = jnp.float16
SIDE = 4
AXES = ("blk", "group")
LANES = 128
LOG2_E = 1.4426950408889634
TAIL = 16
CONTRACT_LAST = (((1,), (1,)), ((), ()))
CONTRACT_FIRST = (((0,), (0,)), ((), ()))


def place(x, y, z, core):
    return (y * 2 + x % 2) * 16 + (z * 2 + x // 2) * 2 + core


def pairs(move):
    found = []
    for x in range(SIDE):
        for y in range(SIDE):
            for z in range(SIDE):
                for core in range(2):
                    found.append((place(x, y, z, core), place(*move(x, y, z, core))))
    return found


def send(values, move):
    return lax.ppermute(values, AXES, pairs(move))


def pair_move(x, y, z, core):
    return (x ^ 1 if core == 0 else 3 - x, y, z, core)


def column_move(x, y, z, core):
    return (3 - x if core == 0 else x ^ 1, y, z, core)


def to_sibling(x, y, z, core):
    return (x, y, z, 1 - core)


def pair_step(step):
    return lambda x, y, z, core: (
        (x, y, (z + step) % SIDE, core) if core == 0 else (x, (y + step) % SIDE, z, core)
    )


def column_step(step):
    return lambda x, y, z, core: (
        (x, (y + step) % SIDE, z, core) if core == 0 else (x, y, (z + step) % SIDE, core)
    )


STEPS = (1, 3, 2)


def on_core():
    return lax.rem(lax.axis_index("group"), 2)


def row_norm_of(wide):
    return jnp.sqrt(jnp.sum(wide * wide, axis=1, keepdims=True) + 1e-06)


def column_of(weight_row, width):
    return jnp.transpose(jnp.broadcast_to(weight_row, (width, weight_row.shape[1])))


def prepare_kernel(img_ref, txt_ref, wgt_ref, pair_out, column_out):
    rows, width = img_ref.shape
    img = img_ref[...].astype(F32)
    img = (img / row_norm_of(img)).astype(BF16)
    txt = txt_ref[...].astype(F32)
    txt = (txt / row_norm_of(txt)).astype(BF16)
    here = pl.ds(0, rows)
    for out in (pair_out, column_out):
        out[pl.ds(rows, TAIL), :] = jnp.zeros((TAIL, width), BF16)
        out[pl.ds(rows, TAIL), pl.ds(0, rows)] = jnp.broadcast_to(wgt_ref[...], (TAIL, rows))

    @pl.when(on_core() == 0)
    def _():
        pair_out[here, :] = img
        column_out[here, :] = txt

    @pl.when(on_core() == 1)
    def _():
        pair_out[here, :] = txt
        column_out[here, :] = img


def join_kernel(log_scale_ref, bias_ref, *refs):
    pair_refs, column_refs, (pair_out, column_out, given) = refs[:2], refs[2:6], refs[6:]
    given[0:1, :] = jnp.exp(jnp.full((1, LANES), log_scale_ref[0], F32))
    given[1:2, :] = jnp.full((1, LANES), bias_ref[0], F32)
    for blocks, out in ((pair_refs, pair_out), (column_refs, column_out)):
        rows = blocks[0].shape[0] - TAIL
        tail = pl.ds(len(blocks) * rows, TAIL)
        out[tail, :] = jnp.zeros((TAIL, out.shape[1]), BF16)
        for index, block in enumerate(blocks):
            out[pl.ds(index * rows, rows), :] = block[pl.ds(0, rows), :]
            out[tail, pl.ds(index * rows, rows)] = block[pl.ds(rows, TAIL), pl.ds(0, rows)]


def weights_of(block, rows, first):
    return block[pl.ds(2 * rows, TAIL), :][0:1, first : first + rows].astype(F32)


def take_pairs(blocks, rows_out, wgt_out):
    rows = rows_out.shape[0] // (2 * SIDE)
    for step, block in enumerate(blocks):
        for chip in range(2):
            there = pl.ds((chip * SIDE + step) * rows, rows)
            rows_out[there, :] = block[pl.ds(chip * rows, rows), :]
            if wgt_out is not None:
                wgt_out[there, :] = column_of(weights_of(block, rows, chip * rows), LANES)


def take_columns(blocks, rows_out, wgt_out):
    span = rows_out.shape[0] // len(blocks)
    for index, block in enumerate(blocks):
        there = pl.ds(index * span, span)
        rows_out[there, :] = block[pl.ds(0, span), :]
        if wgt_out is not None:
            weight = block[pl.ds(span, TAIL), :][0:1, :span].astype(F32)
            wgt_out[there, :] = column_of(weight, LANES)


def score_part(img_all, wgt_all, txt_all, scale, bias, first, coef_out, weighted_out, grad_out, sums_out):
    count, width = img_all.shape
    scale_two, bias_two = scale * LOG2_E, bias * LOG2_E
    span = 256
    rows = 128
    zero = jnp.zeros((8, LANES), F32)
    loss, diff, score = zero, zero, zero
    same = lax.broadcasted_iota(jnp.int32, (rows, LANES), 0) == lax.broadcasted_iota(
        jnp.int32, (rows, LANES), 1
    )

    def fold(values):
        return jnp.sum(values.reshape(-1, 8, LANES), axis=0)

    def scores_of(part):
        img = img_all[pl.ds(span * part, span), :]
        return lax.dot_general(img, txt_all[...], CONTRACT_LAST, preferred_element_type=F32)

    def gradient_of(part):
        here = pl.ds(span * part, span)
        there = pl.ds(first + span * part, span)
        grad_out[here, :] = jnp.dot(coef_out[there, :], txt_all[...], preferred_element_type=F32)

    parts = count // span
    scores = scores_of(0)
    for part in range(parts):
        next_scores = scores_of(part + 1) if part + 1 < parts else None
        if part:
            gradient_of(part - 1)
        here = pl.ds(span * part, span)
        there = pl.ds(first + span * part, span)
        weight = wgt_all[here, :]
        weighted_out[there, :] = (
            img_all[here, :].astype(F32) * jnp.tile(weight, (1, width // LANES))
        ).astype(BF16)
        for tile in range(scores.shape[1] // LANES):
            score_tile = scores[:, tile * LANES : (tile + 1) * LANES]
            grown = jnp.exp2(score_tile * scale_two + bias_two)
            beyond = 1.0 + grown
            diffs = grown / beyond
            if first == 0 and part == 0 and tile == 0:
                diffs = jnp.concatenate(
                    [jnp.where(same, diffs[:rows] - 1.0, diffs[:rows]), diffs[rows:]], axis=0
                )
                matched = jnp.where(same, score_tile[:rows] * scale + bias, 0.0)
                loss = loss - fold(matched * weight[:rows])
            coef_out[there, pl.ds(tile * LANES, LANES)] = diffs.astype(BF16)
            if tile == 0:
                over, diff_row, score_row = grown, diffs, diffs * score_tile
            else:
                over = over * beyond + grown
                diff_row = diff_row + diffs
                score_row = score_row + diffs * score_tile
        loss = loss + fold(jnp.log1p(over) * weight)
        diff = diff + fold(diff_row * weight)
        score = score + fold(score_row * weight)
        scores = next_scores
    gradient_of(parts - 1)
    sums_out[0] = loss
    sums_out[1] = score
    sums_out[2] = diff


def own_kernel(given, *refs):
    pair_refs, column_refs = refs[:4], refs[4:6]
    grad_out, coef_out, weighted_out, sums_out, txt_all, img_all, wgt_all = refs[6:]

    @pl.when(on_core() == 0)
    def _():
        take_pairs(pair_refs, img_all, wgt_all)
        take_columns(column_refs, txt_all, None)

    @pl.when(on_core() == 1)
    def _():
        take_columns(column_refs, img_all, wgt_all)
        take_pairs(pair_refs, txt_all, None)

    score_part(
        img_all, wgt_all, txt_all, given[0:1, :], given[1:2, :], 0, coef_out, weighted_out, grad_out, sums_out
    )


def sibling_kernel(chip, given, *refs):
    pair_refs, column_ref, txt_all = refs[:4], refs[4], refs[5]
    grad_out, coef_out, weighted_out, sums_out, img_all, wgt_all = refs[8:]
    span = img_all.shape[0]
    rows = span // SIDE

    @pl.when(on_core() == 0)
    def _():
        take_columns((column_ref,), img_all, wgt_all)

    @pl.when(on_core() == 1)
    def _():
        for step, block in enumerate(pair_refs):
            there = pl.ds(step * rows, rows)
            img_all[there, :] = block[pl.ds(chip * rows, rows), :]
            wgt_all[there, :] = column_of(weights_of(block, rows, chip * rows), LANES)

    score_part(
        img_all, wgt_all, txt_all, given[0:1, :], given[1:2, :], (2 + chip) * span, coef_out, weighted_out, grad_out, sums_out
    )


def text_kernel(*refs):
    sums_refs, wgt_ref, coef, weighted = refs[:3], *refs[3:6]
    near_out, far_out, sums_out = refs[6:]
    span = near_out.shape[0]
    for chip, out in enumerate((near_out, far_out)):
        here = pl.ds(chip * span, span)
        out[...] = lax.dot_general(
            coef[:, here], weighted[...], CONTRACT_FIRST, preferred_element_type=F32
        )
    lane = lax.broadcasted_iota(jnp.int32, (1, LANES), 1)
    row = jnp.where(lane == 3, jnp.sum(wgt_ref[...].astype(F32), axis=1, keepdims=True), 0.0)
    for kind in range(3):
        part = jnp.sum(sum(ref[kind] for ref in sums_refs), axis=0, keepdims=True)
        row = row + jnp.where(lane == kind, jnp.sum(part, axis=1, keepdims=True), 0.0)
    sums_out[...] = jnp.broadcast_to(row, sums_out.shape)


def merge_kernel(own_grad, near_moved, far_moved, near_txt, far_txt, *outs):
    pair_keep, pair_send, column_keep, column_send = outs
    span = near_txt.shape[0]
    rows = span // SIDE

    def put_pair(chip, step, values):
        there = pl.ds(chip * rows, rows)
        if step == 0:
            pair_keep[there, :] = values
        else:
            pair_send[step - 1, there, :] = values

    for chip, (moved, txt, column) in enumerate(
        ((near_moved, near_txt, column_keep), (far_moved, far_txt, column_send))
    ):
        for step in range(SIDE):
            here = pl.ds(step * rows, rows)
            img_here = pl.ds(chip * span + step * rows, rows)

            @pl.when(on_core() == 0)
            def _():
                put_pair(chip, step, own_grad[img_here, :] + moved[here, :])
                column[here, :] = txt[here, :]

            @pl.when(on_core() == 1)
            def _():
                put_pair(chip, step, txt[here, :])
                column[here, :] = own_grad[img_here, :] + moved[here, :]


def finish_kernel(
    given, sums_ref, img_ref, txt_ref, wgt_ref, pair_sum, column_sum, img_out, txt_out, scalar_out
):
    rows, width = img_ref.shape
    scale = given[0:1, :]
    lane = lax.broadcasted_iota(jnp.int32, (1, LANES), 1)
    sums = jnp.sum(sums_ref[...], axis=0, keepdims=True)
    total = jnp.sum(jnp.where(lane == 3, sums, 0.0), axis=1, keepdims=True)
    pair_count = float(rows * 2 * SIDE**3)
    factor = jnp.tile(scale / total, (1, width // LANES))
    first = on_core() == 0

    def back(gradient, values):
        norm = row_norm_of(values)
        unit = values / norm
        inner = jnp.sum(unit * gradient, axis=1, keepdims=True)
        return pair_count * (gradient - unit * inner) / norm

    weight = jnp.tile(column_of(wgt_ref[...].astype(F32), LANES), (1, width // LANES))
    img_sum = jnp.where(first, pair_sum[...], column_sum[...])
    txt_sum = jnp.where(first, column_sum[...], pair_sum[...])
    img_out[...] = back(factor * weight * img_sum, img_ref[...].astype(F32))
    txt_out[...] = back(factor * txt_sum, txt_ref[...].astype(F32))
    ratio = jnp.where(lane == 1, scale, 1.0) * sums / total
    for kind in range(3):
        scalar_out[kind] = jnp.sum(jnp.where(lane == kind, ratio, 0.0))


VMEM_MIB = 24
IN_VMEM = pl.BlockSpec(memory_space=pltpu.VMEM)
IN_SMEM = pl.BlockSpec(memory_space=pltpu.SMEM)


def call(kernel, shapes, scalars, arrays, flops, moved, scratch=(), limit=16, aliases=None):
    return pl.pallas_call(
        kernel,
        out_shape=[jax.ShapeDtypeStruct(shape, kind) for shape, kind in shapes],
        in_specs=[IN_SMEM] * len(scalars) + [IN_VMEM] * len(arrays),
        out_specs=[IN_SMEM if len(shape) == 1 else IN_VMEM for shape, kind in shapes],
        scratch_shapes=list(scratch),
        input_output_aliases=aliases or {},
        compiler_params=pltpu.CompilerParams(vmem_limit_bytes=limit * 2**20),
        cost_estimate=pl.CostEstimate(flops=flops, bytes_accessed=moved, transcendentals=0),
    )(*scalars, *arrays)


def body(image_embeds, text_embeds, pair_weights, log_scale, bias):
    rows, width = image_embeds.shape
    span, tall = 2 * rows, 2 * SIDE * rows
    devices = 2 * SIDE**3
    weight_row = pair_weights.reshape(1, rows)
    pair_own, column_own = call(
        prepare_kernel,
        [((rows + TAIL, width), BF16)] * 2,
        [],
        [image_embeds, text_embeds, weight_row],
        2 * 8 * rows * width,
        8 * rows * width,
    )
    column_near = [column_own] + [send(column_own, column_step(step)) for step in STEPS]
    pair_near = [pair_own, send(pair_own, pair_move)]
    pair_all, column_all, given = call(
        join_kernel,
        [((span + TAIL, width), BF16), ((SIDE * rows + TAIL, width), BF16), ((8, LANES), F32)],
        [log_scale, bias],
        pair_near + column_near,
        1,
        24 * rows * width,
    )
    pairs_in = [pair_all] + [send(pair_all, pair_step(step)) for step in STEPS]
    columns_in = [column_all, send(column_all, column_move)]
    pairs_sib = [send(block, to_sibling) for block in pairs_in]
    columns_sib = [send(block, to_sibling) for block in columns_in]
    half = 4 * tall * tall * width
    flat = (tall, width)
    sums_shape = ((3, 8, LANES), F32)

    def images_kept(count):
        return [pltpu.VMEM((count, width), BF16), pltpu.VMEM((count, LANES), F32)]

    shared = [((2 * tall, tall), BF16), ((2 * tall, width), BF16)]
    own_grad, coef, weighted, own_sums, txt_all = call(
        own_kernel,
        [(flat, F32)] + shared + [sums_shape, (flat, BF16)],
        [],
        [given] + pairs_in + columns_in,
        half,
        16 * tall * width,
        images_kept(tall),
        VMEM_MIB,
    )
    moved, sums = [], [own_sums]
    for chip in range(2):
        count = tall // 2
        sib_grad, coef, weighted, sib_sums = call(
            functools.partial(sibling_kernel, chip),
            [((count, width), F32)] + shared + [sums_shape],
            [],
            [given] + pairs_sib + [columns_sib[chip], txt_all, coef, weighted],
            half // 2,
            8 * tall * width,
            images_kept(count),
            VMEM_MIB,
            {7: 1, 8: 2},
        )
        moved.append(send(sib_grad, to_sibling))
        sums.append(sib_sums)
    near_txt, far_txt, sums = call(
        text_kernel,
        [((SIDE * rows, width), F32)] * 2 + [((devices, LANES), F32)],
        [],
        sums + [weight_row, coef, weighted],
        half,
        12 * tall * width,
        (),
        VMEM_MIB,
    )
    pair_keep, pair_send, column_keep, column_send = call(
        merge_kernel,
        [
            ((span, width), F32),
            ((SIDE - 1, span, width), F32),
            ((SIDE * rows, width), F32),
            ((SIDE * rows, width), F32),
        ],
        [],
        [own_grad] + moved + [near_txt, far_txt],
        1,
        24 * tall * width,
    )
    column_sum = column_keep + send(column_send.astype(SEND), column_move).astype(F32)
    pair_sum = pair_keep
    for index, step in enumerate(STEPS):
        pair_sum = pair_sum + send(pair_send[index].astype(SEND), pair_step(-step)).astype(F32)
    all_sums = lax.all_to_all(sums, AXES, 0, 0, tiled=True)
    pair_last = pair_sum[:rows] + send(pair_sum[rows:].astype(SEND), pair_move).astype(F32)
    column_last = column_sum[:rows]
    for index, step in enumerate(STEPS):
        block = column_sum[(index + 1) * rows : (index + 2) * rows]
        column_last = column_last + send(block.astype(SEND), column_step(-step)).astype(F32)
    grad_image, grad_text, scalars = call(
        finish_kernel,
        [((rows, width), F32), ((rows, width), F32), ((3,), F32)],
        [],
        [given, all_sums, image_embeds, text_embeds, weight_row, pair_last, column_last],
        2 * 12 * rows * width,
        24 * rows * width,
    )
    return grad_image, grad_text, scalars


def solution(mesh):
    placed = (P(AXES, None), P(AXES, None), P(AXES), P(), P())
    return jax.shard_map(
        body,
        mesh=mesh,
        in_specs=placed,
        out_specs=(P(AXES, None), P(AXES, None), P()),
        check_vma=False,
    )
```

time: 85 us -> 83.1 us (0.978)
  waiting for transfers between devices: 18.9 us -> 16.5 us
    ppermute x23 -> x24, waiting for transfers between devices: 18.9 us -> 16.5 us  [send(): return lax.ppermute(values, AXES, pairs(move))]
    pallas_call x6 -> x8, Pallas kernels: 15.5 us -> 15.9 us  [call(): pl.pallas_call(kernel, out_shape=[jax.ShapeDtypeStruct(shape, kind) for s...]
    ppermute x23 -> x24, starting transfers between devices: 31.2 us -> 31.6 us  [send(): return lax.ppermute(values, AXES, pairs(move))]
  transfers between devices with their start and end apart: 24 -> 25, of which waited for: 12 -> 9; matrix products, arithmetic and copies ran while one was open for 3% -> 4% of each run, Pallas kernels for 6% -> 17%
where the time goes in v1:
time: 83.1 us; the launch traced here: 81.6 us
  starting transfers between devices  40.3 us (48%)
  waiting for transfers between devices  16.5 us (20%)
  Pallas kernels  15.9 us (19%)
  local copies, waits for them, and re-layouts  3.69 us (4%)
  other arithmetic  2.95 us (4%)
  between operations  2.31 us (3%)
    ppermute x24, starting transfers between devices, send(): return lax.ppermute(values, AXES, pairs(move))  31.6 us
    ppermute x24, waiting for transfers between devices, send(): return lax.ppermute(values, AXES, pairs(move))  16.5 us
    pallas_call x8, Pallas kernels, call(): pl.pallas_call(kernel, out_shape=[jax.ShapeDtypeStruct(shape, kind) for s...  15.9 us
    all_to_all x1, starting transfers between devices, body(): all_sums = lax.all_to_all(sums, AXES, 0, 0, tiled=True)  8.71 us
    unnamed x12, local copies, waits for them, and re-layouts  2.52 us
  transfers between devices with their start and end apart: 25, of which 9 were waited for; matrix products, arithmetic and copies ran while one was open for 4% of the time, Pallas kernels for 17%

profile of v1, /device:TPU:1, one launch (start us, length us, event | category | flops | bytes accessed | tf_op | source)
XLA Modules:
  0.0 81.6 jit_solution(3388533974099789163)
XLA Ops:
  3.4 3.4 %collective-permute-start = (bf16[144,768]{1,0:T(8,128)(2,1)S(1)}, bf16[144,768]{1,0:T(8,128)(2,1)S(1)}, u32[]{:S(2)}, u32[]{:S(2)}) collective-permute-start(bf16[144,768]{1,0:T(8,128)(2,1)S(1)} %get-tuple-element.28.refs_0_), channel_id=1, source_target_pairs={{0,16},{1,19},{4,20},{5,23},{8,24},{9,27},{12,28},{13,31},{32,48},... | collective-permute-start | bytes 663560 | tf_op jit(solution)/shard_map/ppermute | solution.py:37
  6.8 3.6 %collective-permute-start.3 = (bf16[144,768]{1,0:T(8,128)(2,1)S(1)}, bf16[144,768]{1,0:T(8,128)(2,1)S(1)}, u32[]{:S(2)}, u32[]{:S(2)}) collective-permute-start(bf16[144,768]{1,0:T(8,128)(2,1)S(1)} %get-tuple-element.29.refs_2_), channel_id=1, source_target_pairs={{0,64},{1,9},{4,68},{5,13},{8,72},{9,1},{12,76},{13,5},{32,96},{33... | collective-permute-start | bytes 663560 | tf_op jit(solution)/shard_map/ppermute | solution.py:37
  10.8 1.0 %collective-permute-start.1 = (bf16[144,768]{1,0:T(8,128)(2,1)S(1)}, bf16[144,768]{1,0:T(8,128)(2,1)S(1)}, u32[]{:S(2)}, u32[]{:S(2)}) collective-permute-start(bf16[144,768]{1,0:T(8,128)(2,1)S(1)} %get-tuple-element.29.refs_2_), channel_id=1, source_target_pairs={{0,32},{1,5},{4,36},{5,9},{8,40},{9,13},{12,44},{13,1},{32,64},{33... | collective-permute-start | bytes 663560 | tf_op jit(solution)/shard_map/ppermute | solution.py:37
  13.7 3.4 %collective-permute-done.2.refs_4_ = bf16[144,768]{1,0:T(8,128)(2,1)S(1)} collective-permute-done((bf16[144,768]{1,0:T(8,128)(2,1)S(1)}, bf16[144,768]{1,0:T(8,128)(2,1)S(1)}, u32[]{:S(2)}, u32[]{:S(2)}) %collective-permute-start.2) | collective-permute-done | bytes 221216 | tf_op jit(solution)/shard_map/ppermute | solution.py:37
  17.3 2.8 %collective-permute-start.8 = (bf16[272,768]{1,0:T(8,128)(2,1)S(1)}, bf16[272,768]{1,0:T(8,128)(2,1)S(1)}, u32[]{:S(2)}, u32[]{:S(2)}) collective-permute-start(bf16[272,768]{1,0:T(8,128)(2,1)S(1)} %get-tuple-element.31.refs_0_), channel_id=1, source_target_pairs={{0,1},{1,0},{4,5},{5,4},{8,9},{9,8},{12,13},{13,12},{32,33},{33,32... | collective-permute-start | bytes 1253384 | tf_op jit(solution)/shard_map/ppermute | solution.py:37
  20.1 1.3 %collective-permute-start.6 = (bf16[272,768]{1,0:T(8,128)(2,1)S(1)}, bf16[272,768]{1,0:T(8,128)(2,1)S(1)}, u32[]{:S(2)}, u32[]{:S(2)}) collective-permute-start(bf16[272,768]{1,0:T(8,128)(2,1)S(1)} %get-tuple-element.31.refs_0_), channel_id=1, source_target_pairs={{0,8},{1,65},{4,12},{5,69},{8,0},{9,73},{12,4},{13,77},{32,40},{33... | collective-permute-start | bytes 1253384 | tf_op jit(solution)/shard_map/ppermute | solution.py:37
  22.9 3.1 %collective-permute-start.12 = (bf16[528,768]{1,0:T(8,128)(2,1)S(1)}, bf16[528,768]{1,0:T(8,128)(2,1)S(1)}, u32[]{:S(2)}, u32[]{:S(2)}) collective-permute-start(bf16[528,768]{1,0:T(8,128)(2,1)S(1)} %get-tuple-element.32.refs_4_), channel_id=1, source_target_pairs={{0,1},{1,0},{4,5},{5,4},{8,9},{9,8},{12,13},{13,12},{32,33},{33,32... | collective-permute-start | bytes 2433032 | tf_op jit(solution)/shard_map/ppermute | solution.py:37
  26.0 2.7 %collective-permute-done.7.refs_5_ = bf16[528,768]{1,0:T(8,128)(2,1)S(1)} collective-permute-done((bf16[528,768]{1,0:T(8,128)(2,1)S(1)}, bf16[528,768]{1,0:T(8,128)(2,1)S(1)}, u32[]{:S(2)}, u32[]{:S(2)}) %collective-permute-start.7) | collective-permute-done | bytes 811040 | tf_op jit(solution)/shard_map/ppermute | solution.py:37
  28.7 2.8 %collective-permute-start.13 = (bf16[528,768]{1,0:T(8,128)(2,1)S(1)}, bf16[528,768]{1,0:T(8,128)(2,1)S(1)}, u32[]{:S(2)}, u32[]{:S(2)}) collective-permute-start(bf16[528,768]{1,0:T(8,128)(2,1)S(1)} %collective-permute-done.7.refs_5_), channel_id=1, source_target_pairs={{0,1},{1,0},{4,5},{5,4},{8,9},{9,8},{12,13},{13,12},{32,33},{33,32... | collective-permute-start | bytes 2433032 | tf_op jit(solution)/shard_map/ppermute | solution.py:37
  32.1 3.5 %collective-permute-start.10 = (bf16[272,768]{1,0:T(8,128)(2,1)S(1)}, bf16[272,768]{1,0:T(8,128)(2,1)S(1)}, u32[]{:S(2)}, u32[]{:S(2)}) collective-permute-start(bf16[272,768]{1,0:T(8,128)(2,1)S(1)} %collective-permute-done.5.refs_2_), channel_id=1, source_target_pairs={{0,1},{1,0},{4,5},{5,4},{8,9},{9,8},{12,13},{13,12},{32,33},{33,32... | collective-permute-start | bytes 1253384 | tf_op jit(solution)/shard_map/ppermute | solution.py:37
  35.5 4.3 %shard_map.78 = (f32[1024,768]{1,0:T(8,128)S(1)}, bf16[2048,1024]{1,0:T(8,128)(2,1)S(1)}, bf16[2048,768]{1,0:T(8,128)(2,1)S(1)}, f32[3,8,128]{2,1,0:T(8,128)S(1)}, bf16[1024,768]{1,0:T(8,128)(2,1)S(1)}) custom-call(f32[8,128]{1,0:T(8,128)S(1)} %get-tuple-element.30.given, bf16[272,768]{1,0:T(8,128)(2,1)S(1)} %get-tuple-element.31.refs_0_, ...), custom_call_target="tpu_custom_call" | custom-call | flops 3221225472 | bytes 12582912 | tf_op jit(solution)/shard_map/pallas_call | solution.py:323
  39.9 2.6 %shard_map.79 = (f32[512,768]{1,0:T(8,128)S(1)}, bf16[2048,1024]{1,0:T(8,128)(2,1)S(1)}, bf16[2048,768]{1,0:T(8,128)(2,1)S(1)}, f32[3,8,128]{2,1,0:T(8,128)S(1)}) custom-call(f32[8,128]{1,0:T(8,128)S(1)} %get-tuple-element.30.given, bf16[272,768]{1,0:T(8,128)(2,1)S(1)} %collective-permute-done.8.refs_0_, ...), custom_call_target="tpu_custom_call", output_to_operand_aliasing={{1}: (7, {}), {2}: (8, {})} | custom-call | flops 1610612736 | bytes 6291456 | tf_op jit(solution)/shard_map/pallas_call | solution.py:323
  43.1 2.8 %shard_map.80 = (f32[512,768]{1,0:T(8,128)S(1)}, bf16[2048,1024]{1,0:T(8,128)(2,1)S(1)}, bf16[2048,768]{1,0:T(8,128)(2,1)S(1)}, f32[3,8,128]{2,1,0:T(8,128)S(1)}) custom-call(f32[8,128]{1,0:T(8,128)S(1)} %get-tuple-element.30.given, bf16[272,768]{1,0:T(8,128)(2,1)S(1)} %collective-permute-done.8.refs_0_, ...), custom_call_target="tpu_custom_call", output_to_operand_aliasing={{1}: (7, {}), {2}: (8, {})} | custom-call | flops 1610612736 | bytes 6291456 | tf_op jit(solution)/shard_map/pallas_call | solution.py:323
  46.0 4.0 %shard_map.81 = (f32[512,768]{1,0:T(8,128)S(1)}, f32[512,768]{1,0:T(8,128)S(1)}, f32[128,128]{1,0:T(8,128)}) custom-call(f32[3,8,128]{2,1,0:T(8,128)S(1)} %get-tuple-element.33.refs_0_, f32[3,8,128]{2,1,0:T(8,128)S(1)} %get-tuple-element.37.refs_1_, f32[3,8,128]{2,1,0:T(8,128)S(1)} %get-tuple-element.40.refs_2_, bf16[1,128]{1,0:T(2,128)(2,1)S(1)} %bitcast.13, ...), custom_call_target="tpu_custom_call" | custom-call | flops 3221225472 | bytes 9437184 | tf_op jit(solution)/shard_map/pallas_call | solution.py:323
  50.8 1.1 %slice_bitcast_fusion.2 = (f16[256,768]{1,0:T(8,128)(2,1)}, f16[256,768]{1,0:T(8,128)(2,1)}, f16[256,768]{1,0:T(8,128)(2,1)}) fusion(f16[3,256,768]{2,1,0:T(8,128)(2,1)S(1)} %convert.13), kind=kLoop, calls=%fused_computation.9 | loop fusion | bytes 2359296 | tf_op jit(solution)/shard_map/convert_element_type | solution.py:422
  51.9 1.2 %collective-permute-start.16 = (f16[256,768]{1,0:T(8,128)(2,1)}, f16[256,768]{1,0:T(8,128)(2,1)}, u32[]{:S(2)}, u32[]{:S(2)}) collective-permute-start(f16[256,768]{1,0:T(8,128)(2,1)} %get-tuple-element.55), channel_id=1, source_target_pairs={{0,12},{1,97},{4,0},{5,101},{8,4},{9,105},{12,8},{13,109},{32,44},... | collective-permute-start | bytes 1179656 | tf_op jit(solution)/shard_map/ppermute | solution.py:37
  55.3 8.7 %all-to-all-start = ((f32[128,1,128]{2,1,0:T(1,128)}), f32[128,1,128]{2,1,0:T(1,128)S(1)}, u32[]{:S(2)}, u32[]{:S(2)}) async-start(f32[128,1,128]{2,1,0:T(1,128)} %bitcast.2), calls=%async_computation | async-start | bytes 131072 | tf_op jit(solution)/shard_map/all_to_all | solution.py:423
  64.1 1.9 %collective-permute-done.17 = f16[256,768]{1,0:T(8,128)(2,1)} collective-permute-done((f16[256,768]{1,0:T(8,128)(2,1)}, f16[256,768]{1,0:T(8,128)(2,1)}, u32[]{:S(2)}, u32[]{:S(2)}) %collective-permute-start.17) | collective-permute-done | bytes 393248 | tf_op jit(solution)/shard_map/ppermute | solution.py:37
  66.0 1.4 %convert_add_fusion.1 = f32[256,768]{1,0:T(8,128)S(1)} fusion(f16[256,768]{1,0:T(8,128)(2,1)} %collective-permute-done.18, f16[256,768]{1,0:T(8,128)(2,1)} %collective-permute-done.17, f32[256,768]{1,0:T(8,128)S(1)} %get-tuple-element.49, f16[256,768]{1,0:T(8,128)(2,1)} %collective-permute-done.16), kind=kLoop, calls=%fused_computation.1 | loop fusion | flops 1179648 | bytes 2752512 | tf_op jit(solution)/shard_map/add | solution.py:422
  68.7 3.0 %collective-permute-start.21 = (f16[128,768]{1,0:T(8,128)(2,1)S(1)}, f16[128,768]{1,0:T(8,128)(2,1)S(1)}, u32[]{:S(2)}, u32[]{:S(2)}) collective-permute-start(f16[128,768]{1,0:T(8,128)(2,1)S(1)} %get-tuple-element.58), channel_id=1, source_target_pairs={{0,96},{1,13},{4,100},{5,1},{8,104},{9,5},{12,108},{13,9},{32,0},{... | collective-permute-start | bytes 589832 | tf_op jit(solution)/shard_map/ppermute | solution.py:37
  73.5 3.0 %collective-permute-done.21 = f16[128,768]{1,0:T(8,128)(2,1)S(1)} collective-permute-done((f16[128,768]{1,0:T(8,128)(2,1)S(1)}, f16[128,768]{1,0:T(8,128)(2,1)S(1)}, u32[]{:S(2)}, u32[]{:S(2)}) %collective-permute-start.21) | collective-permute-done | bytes 196640 | tf_op jit(solution)/shard_map/ppermute | solution.py:37
  76.5 1.6 %collective-permute-done.23 = f16[128,768]{1,0:T(8,128)(2,1)S(1)} collective-permute-done((f16[128,768]{1,0:T(8,128)(2,1)S(1)}, f16[128,768]{1,0:T(8,128)(2,1)S(1)}, u32[]{:S(2)}, u32[]{:S(2)}) %collective-permute-start.23) | collective-permute-done | bytes 196640 | tf_op jit(solution)/shard_map/ppermute | solution.py:37
  78.1 1.9 %collective-permute-done.22 = f16[128,768]{1,0:T(8,128)(2,1)S(1)} collective-permute-done((f16[128,768]{1,0:T(8,128)(2,1)S(1)}, f16[128,768]{1,0:T(8,128)(2,1)S(1)}, u32[]{:S(2)}, u32[]{:S(2)}) %collective-permute-start.22) | collective-permute-done | bytes 196640 | tf_op jit(solution)/shard_map/ppermute | solution.py:37
  80.2 1.3 %shard_map.83 = (f32[128,768]{1,0:T(8,128)}, f32[128,768]{1,0:T(8,128)}, f32[3]{0:T(128)}) custom-call(f32[8,128]{1,0:T(8,128)S(1)} %get-tuple-element.30.given, f32[128,128]{1,0:T(8,128)S(1)} %bitcast.11, bf16[128,768]{1,0:T(8,128)(2,1)S(1)} %copy-done.1, bf16[128,768]{1,0:T(8,128)(2,1)S(1)} %copy-done.3, bf16[1,128]{1,0:T(2,128)(2,1)S(1)} %bitcast.14, ...), custom_call_target="tpu_custom_call" | custom-call | flops 2359296 | bytes 2359296 | tf_op jit(solution)/shard_map/pallas_call | solution.py:323
  (55 shorter events, 13.0 us)
Async XLA Ops:
  3.4 9.8 %collective-permute-start = (bf16[144,768]{1,0:T(8,128)(2,1)S(1)}, bf16[144,768]{1,0:T(8,128)(2,1)S(1)}, u32[]{:S(2)}, u32[]{:S(2)}) collective-permute-start(bf16[144,768]{1,0:T(8,128)(2,1)S(1)} %get-tuple-element.28.refs_0_), channel_id=1, source_target_pairs={{0,16},{1,19},{4,20},{5,23},{8,24},{9,27},{12,28},{13,31},{32,48},... | collective-permute-start | bytes 663560 | tf_op jit(solution)/shard_map/ppermute | solution.py:37
  6.8 6.9 %collective-permute-start.3 = (bf16[144,768]{1,0:T(8,128)(2,1)S(1)}, bf16[144,768]{1,0:T(8,128)(2,1)S(1)}, u32[]{:S(2)}, u32[]{:S(2)}) collective-permute-start(bf16[144,768]{1,0:T(8,128)(2,1)S(1)} %get-tuple-element.29.refs_2_), channel_id=1, source_target_pairs={{0,64},{1,9},{4,68},{5,13},{8,72},{9,1},{12,76},{13,5},{32,96},{33... | collective-permute-start | bytes 663560 | tf_op jit(solution)/shard_map/ppermute | solution.py:37
  10.4 6.8 %collective-permute-start.2 = (bf16[144,768]{1,0:T(8,128)(2,1)S(1)}, bf16[144,768]{1,0:T(8,128)(2,1)S(1)}, u32[]{:S(2)}, u32[]{:S(2)}) collective-permute-start(bf16[144,768]{1,0:T(8,128)(2,1)S(1)} %get-tuple-element.29.refs_2_), channel_id=1, source_target_pairs={{0,96},{1,13},{4,100},{5,1},{8,104},{9,5},{12,108},{13,9},{32,0},{... | collective-permute-start | bytes 663560 | tf_op jit(solution)/shard_map/ppermute | solution.py:37
  10.8 6.3 %collective-permute-start.1 = (bf16[144,768]{1,0:T(8,128)(2,1)S(1)}, bf16[144,768]{1,0:T(8,128)(2,1)S(1)}, u32[]{:S(2)}, u32[]{:S(2)}) collective-permute-start(bf16[144,768]{1,0:T(8,128)(2,1)S(1)} %get-tuple-element.29.refs_2_), channel_id=1, source_target_pairs={{0,32},{1,5},{4,36},{5,9},{8,40},{9,13},{12,44},{13,1},{32,64},{33... | collective-permute-start | bytes 663560 | tf_op jit(solution)/shard_map/ppermute | solution.py:37
  17.2 11.5 %collective-permute-start.7 = (bf16[528,768]{1,0:T(8,128)(2,1)S(1)}, bf16[528,768]{1,0:T(8,128)(2,1)S(1)}, u32[]{:S(2)}, u32[]{:S(2)}) collective-permute-start(bf16[528,768]{1,0:T(8,128)(2,1)S(1)} %get-tuple-element.32.refs_4_), channel_id=1, source_target_pairs={{0,18},{1,17},{4,22},{5,21},{8,26},{9,25},{12,30},{13,29},{32,50},... | collective-permute-start | bytes 2433032 | tf_op jit(solution)/shard_map/ppermute | solution.py:37
  17.3 5.6 %collective-permute-start.8 = (bf16[272,768]{1,0:T(8,128)(2,1)S(1)}, bf16[272,768]{1,0:T(8,128)(2,1)S(1)}, u32[]{:S(2)}, u32[]{:S(2)}) collective-permute-start(bf16[272,768]{1,0:T(8,128)(2,1)S(1)} %get-tuple-element.31.refs_0_), channel_id=1, source_target_pairs={{0,1},{1,0},{4,5},{5,4},{8,9},{9,8},{12,13},{13,12},{32,33},{33,32... | collective-permute-start | bytes 1253384 | tf_op jit(solution)/shard_map/ppermute | solution.py:37
  20.1 11.4 %collective-permute-start.6 = (bf16[272,768]{1,0:T(8,128)(2,1)S(1)}, bf16[272,768]{1,0:T(8,128)(2,1)S(1)}, u32[]{:S(2)}, u32[]{:S(2)}) collective-permute-start(bf16[272,768]{1,0:T(8,128)(2,1)S(1)} %get-tuple-element.31.refs_0_), channel_id=1, source_target_pairs={{0,8},{1,65},{4,12},{5,69},{8,0},{9,73},{12,4},{13,77},{32,40},{33... | collective-permute-start | bytes 1253384 | tf_op jit(solution)/shard_map/ppermute | solution.py:37
  21.4 10.6 %collective-permute-start.5 = (bf16[272,768]{1,0:T(8,128)(2,1)S(1)}, bf16[272,768]{1,0:T(8,128)(2,1)S(1)}, u32[]{:S(2)}, u32[]{:S(2)}) collective-permute-start(bf16[272,768]{1,0:T(8,128)(2,1)S(1)} %get-tuple-element.31.refs_0_), channel_id=1, source_target_pairs={{0,12},{1,97},{4,0},{5,101},{8,4},{9,105},{12,8},{13,109},{32,44},... | collective-permute-start | bytes 1253384 | tf_op jit(solution)/shard_map/ppermute | solution.py:37
  22.3 13.2 %collective-permute-start.4 = (bf16[272,768]{1,0:T(8,128)(2,1)S(1)}, bf16[272,768]{1,0:T(8,128)(2,1)S(1)}, u32[]{:S(2)}, u32[]{:S(2)}) collective-permute-start(bf16[272,768]{1,0:T(8,128)(2,1)S(1)} %get-tuple-element.31.refs_0_), channel_id=1, source_target_pairs={{0,4},{1,33},{4,8},{5,37},{8,12},{9,41},{12,0},{13,45},{32,36},{33... | collective-permute-start | bytes 1253384 | tf_op jit(solution)/shard_map/ppermute | solution.py:37
  22.9 17.0 %collective-permute-start.12 = (bf16[528,768]{1,0:T(8,128)(2,1)S(1)}, bf16[528,768]{1,0:T(8,128)(2,1)S(1)}, u32[]{:S(2)}, u32[]{:S(2)}) collective-permute-start(bf16[528,768]{1,0:T(8,128)(2,1)S(1)} %get-tuple-element.32.refs_4_), channel_id=1, source_target_pairs={{0,1},{1,0},{4,5},{5,4},{8,9},{9,8},{12,13},{13,12},{32,33},{33,32... | collective-permute-start | bytes 2433032 | tf_op jit(solution)/shard_map/ppermute | solution.py:37
  28.7 14.5 %collective-permute-start.13 = (bf16[528,768]{1,0:T(8,128)(2,1)S(1)}, bf16[528,768]{1,0:T(8,128)(2,1)S(1)}, u32[]{:S(2)}, u32[]{:S(2)}) collective-permute-start(bf16[528,768]{1,0:T(8,128)(2,1)S(1)} %collective-permute-done.7.refs_5_), channel_id=1, source_target_pairs={{0,1},{1,0},{4,5},{5,4},{8,9},{9,8},{12,13},{13,12},{32,33},{33,32... | collective-permute-start | bytes 2433032 | tf_op jit(solution)/shard_map/ppermute | solution.py:37
  31.5 8.4 %collective-permute-start.11 = (bf16[272,768]{1,0:T(8,128)(2,1)S(1)}, bf16[272,768]{1,0:T(8,128)(2,1)S(1)}, u32[]{:S(2)}, u32[]{:S(2)}) collective-permute-start(bf16[272,768]{1,0:T(8,128)(2,1)S(1)} %collective-permute-done.6.refs_3_), channel_id=1, source_target_pairs={{0,1},{1,0},{4,5},{5,4},{8,9},{9,8},{12,13},{13,12},{32,33},{33,32... | collective-permute-start | bytes 1253384 | tf_op jit(solution)/shard_map/ppermute | solution.py:37
  32.1 7.8 %collective-permute-start.10 = (bf16[272,768]{1,0:T(8,128)(2,1)S(1)}, bf16[272,768]{1,0:T(8,128)(2,1)S(1)}, u32[]{:S(2)}, u32[]{:S(2)}) collective-permute-start(bf16[272,768]{1,0:T(8,128)(2,1)S(1)} %collective-permute-done.5.refs_2_), channel_id=1, source_target_pairs={{0,1},{1,0},{4,5},{5,4},{8,9},{9,8},{12,13},{13,12},{32,33},{33,32... | collective-permute-start | bytes 1253384 | tf_op jit(solution)/shard_map/ppermute | solution.py:37
  35.5 4.4 %collective-permute-start.9 = (bf16[272,768]{1,0:T(8,128)(2,1)S(1)}, bf16[272,768]{1,0:T(8,128)(2,1)S(1)}, u32[]{:S(2)}, u32[]{:S(2)}) collective-permute-start(bf16[272,768]{1,0:T(8,128)(2,1)S(1)} %collective-permute-done.4.refs_1_), channel_id=1, source_target_pairs={{0,1},{1,0},{4,5},{5,4},{8,9},{9,8},{12,13},{13,12},{32,33},{33,32... | collective-permute-start | bytes 1253384 | tf_op jit(solution)/shard_map/ppermute | solution.py:37
  42.6 7.5 %collective-permute-start.14 = (f32[512,768]{1,0:T(8,128)S(1)}, f32[512,768]{1,0:T(8,128)S(1)}, u32[]{:S(2)}, u32[]{:S(2)}) collective-permute-start(f32[512,768]{1,0:T(8,128)S(1)} %get-tuple-element.45), channel_id=1, source_target_pairs={{0,1},{1,0},{4,5},{5,4},{8,9},{9,8},{12,13},{13,12},{32,33},{33,32... | collective-permute-start | bytes 4718600 | tf_op jit(solution)/shard_map/ppermute | solution.py:37
  51.9 12.2 %collective-permute-start.16 = (f16[256,768]{1,0:T(8,128)(2,1)}, f16[256,768]{1,0:T(8,128)(2,1)}, u32[]{:S(2)}, u32[]{:S(2)}) collective-permute-start(f16[256,768]{1,0:T(8,128)(2,1)} %get-tuple-element.55), channel_id=1, source_target_pairs={{0,12},{1,97},{4,0},{5,101},{8,4},{9,105},{12,8},{13,109},{32,44},... | collective-permute-start | bytes 1179656 | tf_op jit(solution)/shard_map/ppermute | solution.py:37
  53.0 11.1 %collective-permute-start.18 = (f16[256,768]{1,0:T(8,128)(2,1)}, f16[256,768]{1,0:T(8,128)(2,1)}, u32[]{:S(2)}, u32[]{:S(2)}) collective-permute-start(f16[256,768]{1,0:T(8,128)(2,1)} %get-tuple-element.56), channel_id=1, source_target_pairs={{0,8},{1,65},{4,12},{5,69},{8,0},{9,73},{12,4},{13,77},{32,40},{33... | collective-permute-start | bytes 1179656 | tf_op jit(solution)/shard_map/ppermute | solution.py:37
  53.5 12.5 %collective-permute-start.17 = (f16[256,768]{1,0:T(8,128)(2,1)}, f16[256,768]{1,0:T(8,128)(2,1)}, u32[]{:S(2)}, u32[]{:S(2)}) collective-permute-start(f16[256,768]{1,0:T(8,128)(2,1)} %get-tuple-element.57), channel_id=1, source_target_pairs={{0,4},{1,33},{4,8},{5,37},{8,12},{9,41},{12,0},{13,45},{32,36},{33... | collective-permute-start | bytes 1179656 | tf_op jit(solution)/shard_map/ppermute | solution.py:37
  55.0 13.3 %collective-permute-start.20 = (f16[512,768]{1,0:T(8,128)(2,1)}, f16[512,768]{1,0:T(8,128)(2,1)S(1)}, u32[]{:S(2)}, u32[]{:S(2)}) collective-permute-start(f16[512,768]{1,0:T(8,128)(2,1)} %convert_element_type.50), channel_id=1, source_target_pairs={{0,18},{1,17},{4,22},{5,21},{8,26},{9,25},{12,30},{13,29},{32,50},... | collective-permute-start | bytes 2359304 | tf_op jit(solution)/shard_map/ppermute | solution.py:37
  55.3 24.8 %all-to-all-start = ((f32[128,1,128]{2,1,0:T(1,128)}), f32[128,1,128]{2,1,0:T(1,128)S(1)}, u32[]{:S(2)}, u32[]{:S(2)}) async-start(f32[128,1,128]{2,1,0:T(1,128)} %bitcast.2), calls=%async_computation | async-start | bytes 131072 | tf_op jit(solution)/shard_map/all_to_all | solution.py:423
  67.4 6.1 %collective-permute-start.19 = (f16[128,768]{1,0:T(8,128)(2,1)S(1)}, f16[128,768]{1,0:T(8,128)(2,1)S(1)}, u32[]{:S(2)}, u32[]{:S(2)}) collective-permute-start(f16[128,768]{1,0:T(8,128)(2,1)S(1)} %slice_convert_fusion), channel_id=1, source_target_pairs={{0,16},{1,19},{4,20},{5,23},{8,24},{9,27},{12,28},{13,31},{32,48},... | collective-permute-start | bytes 589832 | tf_op jit(solution)/shard_map/ppermute | solution.py:37
  68.7 7.8 %collective-permute-start.21 = (f16[128,768]{1,0:T(8,128)(2,1)S(1)}, f16[128,768]{1,0:T(8,128)(2,1)S(1)}, u32[]{:S(2)}, u32[]{:S(2)}) collective-permute-start(f16[128,768]{1,0:T(8,128)(2,1)S(1)} %get-tuple-element.58), channel_id=1, source_target_pairs={{0,96},{1,13},{4,100},{5,1},{8,104},{9,5},{12,108},{13,9},{32,0},{... | collective-permute-start | bytes 589832 | tf_op jit(solution)/shard_map/ppermute | solution.py:37
  71.8 6.4 %collective-permute-start.23 = (f16[128,768]{1,0:T(8,128)(2,1)S(1)}, f16[128,768]{1,0:T(8,128)(2,1)S(1)}, u32[]{:S(2)}, u32[]{:S(2)}) collective-permute-start(f16[128,768]{1,0:T(8,128)(2,1)S(1)} %get-tuple-element.59), channel_id=1, source_target_pairs={{0,64},{1,9},{4,68},{5,13},{8,72},{9,1},{12,76},{13,5},{32,96},{33... | collective-permute-start | bytes 589832 | tf_op jit(solution)/shard_map/ppermute | solution.py:37
  71.9 8.1 %collective-permute-start.22 = (f16[128,768]{1,0:T(8,128)(2,1)S(1)}, f16[128,768]{1,0:T(8,128)(2,1)S(1)}, u32[]{:S(2)}, u32[]{:S(2)}) collective-permute-start(f16[128,768]{1,0:T(8,128)(2,1)S(1)} %get-tuple-element.60), channel_id=1, source_target_pairs={{0,32},{1,5},{4,36},{5,9},{8,40},{9,13},{12,44},{13,1},{32,64},{33... | collective-permute-start | bytes 589832 | tf_op jit(solution)/shard_map/ppermute | solution.py:37
  (7 other events, 32.6 us)

commit v2 on v1

--- a/solution.py
+++ b/solution.py
@@ -61,7 +61,7 @@
     )
 
 
-STEPS = (1, 3, 2)
+STEPS = (2, 3, 1)
 
 
 def on_core():
@@ -286,16 +286,10 @@
                 column[here, :] = own_grad[img_here, :] + moved[here, :]
 
 
-def finish_kernel(
-    given, sums_ref, img_ref, txt_ref, wgt_ref, pair_sum, column_sum, img_out, txt_out, scalar_out
-):
+def back_kernel(given, img_ref, txt_ref, wgt_ref, pair_sum, column_sum, img_out, txt_out):
     rows, width = img_ref.shape
-    scale = given[0:1, :]
-    lane = lax.broadcasted_iota(jnp.int32, (1, LANES), 1)
-    sums = jnp.sum(sums_ref[...], axis=0, keepdims=True)
-    total = jnp.sum(jnp.where(lane == 3, sums, 0.0), axis=1, keepdims=True)
     pair_count = float(rows * 2 * SIDE**3)
-    factor = jnp.tile(scale / total, (1, width // LANES))
+    scale = jnp.tile(given[0:1, :], (1, width // LANES))
     first = on_core() == 0
 
     def back(gradient, values):
@@ -307,14 +301,24 @@
     weight = jnp.tile(column_of(wgt_ref[...].astype(F32), LANES), (1, width // LANES))
     img_sum = jnp.where(first, pair_sum[...], column_sum[...])
     txt_sum = jnp.where(first, column_sum[...], pair_sum[...])
-    img_out[...] = back(factor * weight * img_sum, img_ref[...].astype(F32))
-    txt_out[...] = back(factor * txt_sum, txt_ref[...].astype(F32))
-    ratio = jnp.where(lane == 1, scale, 1.0) * sums / total
+    img_out[...] = back(scale * weight * img_sum, img_ref[...].astype(F32))
+    txt_out[...] = back(scale * txt_sum, txt_ref[...].astype(F32))
+
+
+def finish_kernel(given, sums_ref, img_back, txt_back, img_out, txt_out, scalar_out):
+    lane = lax.broadcasted_iota(jnp.int32, (1, LANES), 1)
+    sums = jnp.sum(sums_ref[...], axis=0, keepdims=True)
+    total = jnp.sum(jnp.where(lane == 3, sums, 0.0), axis=1, keepdims=True)
+    share = 1.0 / total
+    img_out[...] = img_back[...] * share
+    txt_out[...] = txt_back[...] * share
+    ratio = jnp.where(lane == 1, given[0:1, :], 1.0) * sums / total
     for kind in range(3):
         scalar_out[kind] = jnp.sum(jnp.where(lane == kind, ratio, 0.0))
 
 
 VMEM_MIB = 24
+LONG_FLOPS = 4 * 10**10
 IN_VMEM = pl.BlockSpec(memory_space=pltpu.VMEM)
 IN_SMEM = pl.BlockSpec(memory_space=pltpu.SMEM)
 
@@ -417,7 +421,7 @@
         24 * tall * width,
     )
     column_sum = column_keep + send(column_send.astype(SEND), column_move).astype(F32)
-    pair_sum = pair_keep
+    pair_sum = pair_keep + 0.0 * column_sum[0, 0]
     for index, step in enumerate(STEPS):
         pair_sum = pair_sum + send(pair_send[index].astype(SEND), pair_step(-step)).astype(F32)
     all_sums = lax.all_to_all(sums, AXES, 0, 0, tiled=True)
@@ -426,13 +430,21 @@
     for index, step in enumerate(STEPS):
         block = column_sum[(index + 1) * rows : (index + 2) * rows]
         column_last = column_last + send(block.astype(SEND), column_step(-step)).astype(F32)
+    img_back, txt_back = call(
+        back_kernel,
+        [((rows, width), F32)] * 2,
+        [],
+        [given, image_embeds, text_embeds, weight_row, pair_last, column_last],
+        LONG_FLOPS,
+        24 * rows * width,
+    )
     grad_image, grad_text, scalars = call(
         finish_kernel,
         [((rows, width), F32), ((rows, width), F32), ((3,), F32)],
         [],
-        [given, all_sums, image_embeds, text_embeds, weight_row, pair_last, column_last],
-        2 * 12 * rows * width,
-        24 * rows * width,
+        [given, all_sums, img_back, txt_back],
+        2 * rows * width,
+        16 * rows * width,
     )
     return grad_image, grad_text, scalars
 

time: 83.1 us -> 82.7 us (level); the launches traced: 81.6 us -> 82.4 us
  waiting for transfers between devices: 16.5 us -> 13.7 us
  starting transfers between devices: 40.3 us -> 42.4 us
    ppermute x24, waiting for transfers between devices: 16.5 us -> 13.7 us  [send(): return lax.ppermute(values, AXES, pairs(move))]
    ppermute x24, starting transfers between devices: 31.6 us -> 33.9 us  [send(): return lax.ppermute(values, AXES, pairs(move))]
    pallas_call x8 -> x9, Pallas kernels: 15.9 us -> 16.1 us  [call(): pl.pallas_call(kernel, out_shape=[jax.ShapeDtypeStruct(shape, kind) for s...]
  transfers between devices with their start and end apart: 25 -> 25, of which waited for: 9 -> 8; matrix products, arithmetic and copies ran while one was open for 4% -> 4% of each run, Pallas kernels for 17% -> 17%
where the time goes in v2:
time: 82.7 us; the launch traced here: 82.4 us
  starting transfers between devices  42.4 us (51%)
  Pallas kernels  16.1 us (19%)
  waiting for transfers between devices  13.7 us (17%)
  local copies, waits for them, and re-layouts  4.2 us (5%)
  other arithmetic  3.02 us (4%)
  between operations  2.97 us (4%)
    ppermute x24, starting transfers between devices, send(): return lax.ppermute(values, AXES, pairs(move))  33.9 us
    pallas_call x9, Pallas kernels, call(): pl.pallas_call(kernel, out_shape=[jax.ShapeDtypeStruct(shape, kind) for s...  16.1 us
    ppermute x24, waiting for transfers between devices, send(): return lax.ppermute(values, AXES, pairs(move))  13.7 us
    all_to_all x1, starting transfers between devices, body(): all_sums = lax.all_to_all(sums, AXES, 0, 0, tiled=True)  8.5 us
    unnamed x12, local copies, waits for them, and re-layouts  2.52 us
  transfers between devices with their start and end apart: 25, of which 8 were waited for; matrix products, arithmetic and copies ran while one was open for 4% of the time, Pallas kernels for 17%

profile of v2, /device:TPU:1, one launch (start us, length us, event | category | flops | bytes accessed | tf_op | source)
XLA Modules:
  0.0 82.4 jit_solution(15485470812012155337)
XLA Ops:
  3.4 3.4 %collective-permute-start = (bf16[144,768]{1,0:T(8,128)(2,1)S(1)}, bf16[144,768]{1,0:T(8,128)(2,1)S(1)}, u32[]{:S(2)}, u32[]{:S(2)}) collective-permute-start(bf16[144,768]{1,0:T(8,128)(2,1)S(1)} %get-tuple-element.30.refs_0_), channel_id=1, source_target_pairs={{0,16},{1,19},{4,20},{5,23},{8,24},{9,27},{12,28},{13,31},{32,48},... | collective-permute-start | bytes 663560 | tf_op jit(solution)/shard_map/ppermute | solution.py:37
  6.8 1.6 %collective-permute-start.3 = (bf16[144,768]{1,0:T(8,128)(2,1)S(1)}, bf16[144,768]{1,0:T(8,128)(2,1)S(1)}, u32[]{:S(2)}, u32[]{:S(2)}) collective-permute-start(bf16[144,768]{1,0:T(8,128)(2,1)S(1)} %get-tuple-element.31.refs_2_), channel_id=1, source_target_pairs={{0,32},{1,5},{4,36},{5,9},{8,40},{9,13},{12,44},{13,1},{32,64},{33... | collective-permute-start | bytes 663560 | tf_op jit(solution)/shard_map/ppermute | solution.py:37
  8.4 2.1 %collective-permute-start.2 = (bf16[144,768]{1,0:T(8,128)(2,1)S(1)}, bf16[144,768]{1,0:T(8,128)(2,1)S(1)}, u32[]{:S(2)}, u32[]{:S(2)}) collective-permute-start(bf16[144,768]{1,0:T(8,128)(2,1)S(1)} %get-tuple-element.31.refs_2_), channel_id=1, source_target_pairs={{0,96},{1,13},{4,100},{5,1},{8,104},{9,5},{12,108},{13,9},{32,0},{... | collective-permute-start | bytes 663560 | tf_op jit(solution)/shard_map/ppermute | solution.py:37
  13.8 1.9 %collective-permute-done.2.refs_4_ = bf16[144,768]{1,0:T(8,128)(2,1)S(1)} collective-permute-done((bf16[144,768]{1,0:T(8,128)(2,1)S(1)}, bf16[144,768]{1,0:T(8,128)(2,1)S(1)}, u32[]{:S(2)}, u32[]{:S(2)}) %collective-permute-start.2) | collective-permute-done | bytes 221216 | tf_op jit(solution)/shard_map/ppermute | solution.py:37
  15.8 1.6 %collective-permute-done.1.refs_3_ = bf16[144,768]{1,0:T(8,128)(2,1)S(1)} collective-permute-done((bf16[144,768]{1,0:T(8,128)(2,1)S(1)}, bf16[144,768]{1,0:T(8,128)(2,1)S(1)}, u32[]{:S(2)}, u32[]{:S(2)}) %collective-permute-start.1) | collective-permute-done | bytes 221216 | tf_op jit(solution)/shard_map/ppermute | solution.py:37
  17.6 1.9 %collective-permute-start.8 = (bf16[272,768]{1,0:T(8,128)(2,1)S(1)}, bf16[272,768]{1,0:T(8,128)(2,1)S(1)}, u32[]{:S(2)}, u32[]{:S(2)}) collective-permute-start(bf16[272,768]{1,0:T(8,128)(2,1)S(1)} %get-tuple-element.33.refs_0_), channel_id=1, source_target_pairs={{0,1},{1,0},{4,5},{5,4},{8,9},{9,8},{12,13},{13,12},{32,33},{33,32... | collective-permute-start | bytes 1253384 | tf_op jit(solution)/shard_map/ppermute | solution.py:37
  20.6 1.5 %collective-permute-start.5 = (bf16[272,768]{1,0:T(8,128)(2,1)S(1)}, bf16[272,768]{1,0:T(8,128)(2,1)S(1)}, u32[]{:S(2)}, u32[]{:S(2)}) collective-permute-start(bf16[272,768]{1,0:T(8,128)(2,1)S(1)} %get-tuple-element.33.refs_0_), channel_id=1, source_target_pairs={{0,12},{1,97},{4,0},{5,101},{8,4},{9,105},{12,8},{13,109},{32,44},... | collective-permute-start | bytes 1253384 | tf_op jit(solution)/shard_map/ppermute | solution.py:37
  22.6 2.8 %collective-permute-start.12 = (bf16[528,768]{1,0:T(8,128)(2,1)S(1)}, bf16[528,768]{1,0:T(8,128)(2,1)S(1)}, u32[]{:S(2)}, u32[]{:S(2)}) collective-permute-start(bf16[528,768]{1,0:T(8,128)(2,1)S(1)} %get-tuple-element.34.refs_4_), channel_id=1, source_target_pairs={{0,1},{1,0},{4,5},{5,4},{8,9},{9,8},{12,13},{13,12},{32,33},{33,32... | collective-permute-start | bytes 2433032 | tf_op jit(solution)/shard_map/ppermute | solution.py:37
  25.4 3.6 %collective-permute-done.7.refs_5_ = bf16[528,768]{1,0:T(8,128)(2,1)S(1)} collective-permute-done((bf16[528,768]{1,0:T(8,128)(2,1)S(1)}, bf16[528,768]{1,0:T(8,128)(2,1)S(1)}, u32[]{:S(2)}, u32[]{:S(2)}) %collective-permute-start.7) | collective-permute-done | bytes 811040 | tf_op jit(solution)/shard_map/ppermute | solution.py:37
  28.9 1.9 %collective-permute-start.13 = (bf16[528,768]{1,0:T(8,128)(2,1)S(1)}, bf16[528,768]{1,0:T(8,128)(2,1)S(1)}, u32[]{:S(2)}, u32[]{:S(2)}) collective-permute-start(bf16[528,768]{1,0:T(8,128)(2,1)S(1)} %collective-permute-done.7.refs_5_), channel_id=1, source_target_pairs={{0,1},{1,0},{4,5},{5,4},{8,9},{9,8},{12,13},{13,12},{32,33},{33,32... | collective-permute-start | bytes 2433032 | tf_op jit(solution)/shard_map/ppermute | solution.py:37
  31.6 2.0 %collective-permute-start.10 = (bf16[272,768]{1,0:T(8,128)(2,1)S(1)}, bf16[272,768]{1,0:T(8,128)(2,1)S(1)}, u32[]{:S(2)}, u32[]{:S(2)}) collective-permute-start(bf16[272,768]{1,0:T(8,128)(2,1)S(1)} %collective-permute-done.5.refs_2_), channel_id=1, source_target_pairs={{0,1},{1,0},{4,5},{5,4},{8,9},{9,8},{12,13},{13,12},{32,33},{33,32... | collective-permute-start | bytes 1253384 | tf_op jit(solution)/shard_map/ppermute | solution.py:37
  33.6 1.9 %collective-permute-start.9 = (bf16[272,768]{1,0:T(8,128)(2,1)S(1)}, bf16[272,768]{1,0:T(8,128)(2,1)S(1)}, u32[]{:S(2)}, u32[]{:S(2)}) collective-permute-start(bf16[272,768]{1,0:T(8,128)(2,1)S(1)} %collective-permute-done.4.refs_1_), channel_id=1, source_target_pairs={{0,1},{1,0},{4,5},{5,4},{8,9},{9,8},{12,13},{13,12},{32,33},{33,32... | collective-permute-start | bytes 1253384 | tf_op jit(solution)/shard_map/ppermute | solution.py:37
  35.5 4.3 %shard_map.78 = (f32[1024,768]{1,0:T(8,128)S(1)}, bf16[2048,1024]{1,0:T(8,128)(2,1)S(1)}, bf16[2048,768]{1,0:T(8,128)(2,1)S(1)}, f32[3,8,128]{2,1,0:T(8,128)S(1)}, bf16[1024,768]{1,0:T(8,128)(2,1)S(1)}) custom-call(f32[8,128]{1,0:T(8,128)S(1)} %get-tuple-element.32.given, bf16[272,768]{1,0:T(8,128)(2,1)S(1)} %get-tuple-element.33.refs_0_, ...), custom_call_target="tpu_custom_call" | custom-call | flops 3221225472 | bytes 12582912 | tf_op jit(solution)/shard_map/pallas_call | solution.py:327
  39.8 2.6 %shard_map.79 = (f32[512,768]{1,0:T(8,128)S(1)}, bf16[2048,1024]{1,0:T(8,128)(2,1)S(1)}, bf16[2048,768]{1,0:T(8,128)(2,1)S(1)}, f32[3,8,128]{2,1,0:T(8,128)S(1)}) custom-call(f32[8,128]{1,0:T(8,128)S(1)} %get-tuple-element.32.given, bf16[272,768]{1,0:T(8,128)(2,1)S(1)} %collective-permute-done.8.refs_0_, ...), custom_call_target="tpu_custom_call", output_to_operand_aliasing={{1}: (7, {}), {2}: (8, {})} | custom-call | flops 1610612736 | bytes 6291456 | tf_op jit(solution)/shard_map/pallas_call | solution.py:327
  42.6 2.8 %shard_map.80 = (f32[512,768]{1,0:T(8,128)S(1)}, bf16[2048,1024]{1,0:T(8,128)(2,1)S(1)}, bf16[2048,768]{1,0:T(8,128)(2,1)S(1)}, f32[3,8,128]{2,1,0:T(8,128)S(1)}) custom-call(f32[8,128]{1,0:T(8,128)S(1)} %get-tuple-element.32.given, bf16[272,768]{1,0:T(8,128)(2,1)S(1)} %collective-permute-done.8.refs_0_, ...), custom_call_target="tpu_custom_call", output_to_operand_aliasing={{1}: (7, {}), {2}: (8, {})} | custom-call | flops 1610612736 | bytes 6291456 | tf_op jit(solution)/shard_map/pallas_call | solution.py:327
  45.9 4.0 %shard_map.81 = (f32[512,768]{1,0:T(8,128)S(1)}, f32[512,768]{1,0:T(8,128)S(1)}, f32[128,128]{1,0:T(8,128)}) custom-call(f32[3,8,128]{2,1,0:T(8,128)S(1)} %get-tuple-element.35.refs_0_, f32[3,8,128]{2,1,0:T(8,128)S(1)} %get-tuple-element.39.refs_1_, f32[3,8,128]{2,1,0:T(8,128)S(1)} %get-tuple-element.42.refs_2_, bf16[1,128]{1,0:T(2,128)(2,1)S(1)} %bitcast.14, ...), custom_call_target="tpu_custom_call" | custom-call | flops 3221225472 | bytes 9437184 | tf_op jit(solution)/shard_map/pallas_call | solution.py:327
  53.0 1.6 %collective-permute-start.17 = (f16[256,768]{1,0:T(8,128)(2,1)}, f16[256,768]{1,0:T(8,128)(2,1)}, u32[]{:S(2)}, u32[]{:S(2)}) collective-permute-start(f16[256,768]{1,0:T(8,128)(2,1)} %get-tuple-element.59), channel_id=1, source_target_pairs={{0,8},{1,65},{4,12},{5,69},{8,0},{9,73},{12,4},{13,77},{32,40},{33... | collective-permute-start | bytes 1179656 | tf_op jit(solution)/shard_map/ppermute | solution.py:37
  54.7 1.9 %collective-permute-start.19 = (f16[256,768]{1,0:T(8,128)(2,1)}, f16[256,768]{1,0:T(8,128)(2,1)}, u32[]{:S(2)}, u32[]{:S(2)}) collective-permute-start(f16[256,768]{1,0:T(8,128)(2,1)} %get-tuple-element.60), channel_id=1, source_target_pairs={{0,12},{1,97},{4,0},{5,101},{8,4},{9,105},{12,8},{13,109},{32,44},... | collective-permute-start | bytes 1179656 | tf_op jit(solution)/shard_map/ppermute | solution.py:37
  56.6 8.5 %all-to-all-start = ((f32[128,1,128]{2,1,0:T(1,128)}), f32[128,1,128]{2,1,0:T(1,128)S(1)}, u32[]{:S(2)}, u32[]{:S(2)}) async-start(f32[128,1,128]{2,1,0:T(1,128)} %bitcast.2), calls=%async_computation | async-start | bytes 131072 | tf_op jit(solution)/shard_map/all_to_all | solution.py:427
  66.6 1.4 %convert_add_fusion.1 = f32[256,768]{1,0:T(8,128)S(1)} fusion(f16[256,768]{1,0:T(8,128)(2,1)} %collective-permute-done.19, f16[256,768]{1,0:T(8,128)(2,1)} %collective-permute-done.18, f16[256,768]{1,0:T(8,128)(2,1)} %collective-permute-done.17, f32[256,768]{1,0:T(8,128)S(1)} %get-tuple-element.51, f32[]{:T(128)} %bitcast.4), kind=kLoop, calls=%fused_computation.1 | loop fusion | flops 1376256 | bytes 2752516 | tf_op jit(solution)/shard_map/add | solution.py:426
  68.0 2.7 %collective-permute-start.20 = (f16[128,768]{1,0:T(8,128)(2,1)S(1)}, f16[128,768]{1,0:T(8,128)(2,1)S(1)}, u32[]{:S(2)}, u32[]{:S(2)}) collective-permute-start(f16[128,768]{1,0:T(8,128)(2,1)S(1)} %slice_convert_fusion), channel_id=1, source_target_pairs={{0,16},{1,19},{4,20},{5,23},{8,24},{9,27},{12,28},{13,31},{32,48},... | collective-permute-start | bytes 589832 | tf_op jit(solution)/shard_map/ppermute | solution.py:37
  70.8 3.2 %collective-permute-start.21 = (f16[128,768]{1,0:T(8,128)(2,1)S(1)}, f16[128,768]{1,0:T(8,128)(2,1)S(1)}, u32[]{:S(2)}, u32[]{:S(2)}) collective-permute-start(f16[128,768]{1,0:T(8,128)(2,1)S(1)} %get-tuple-element.62), channel_id=1, source_target_pairs={{0,64},{1,9},{4,68},{5,13},{8,72},{9,1},{12,76},{13,5},{32,96},{33... | collective-permute-start | bytes 589832 | tf_op jit(solution)/shard_map/ppermute | solution.py:37
  75.5 1.5 %collective-permute-done.21 = f16[128,768]{1,0:T(8,128)(2,1)S(1)} collective-permute-done((f16[128,768]{1,0:T(8,128)(2,1)S(1)}, f16[128,768]{1,0:T(8,128)(2,1)S(1)}, u32[]{:S(2)}, u32[]{:S(2)}) %collective-permute-start.21) | collective-permute-done | bytes 196640 | tf_op jit(solution)/shard_map/ppermute | solution.py:37
  77.1 3.0 %collective-permute-done.23 = f16[128,768]{1,0:T(8,128)(2,1)S(1)} collective-permute-done((f16[128,768]{1,0:T(8,128)(2,1)S(1)}, f16[128,768]{1,0:T(8,128)(2,1)S(1)}, u32[]{:S(2)}, u32[]{:S(2)}) %collective-permute-start.23) | collective-permute-done | bytes 196640 | tf_op jit(solution)/shard_map/ppermute | solution.py:37
  (57 shorter events, 15.6 us)
Async XLA Ops:
  3.4 9.8 %collective-permute-start = (bf16[144,768]{1,0:T(8,128)(2,1)S(1)}, bf16[144,768]{1,0:T(8,128)(2,1)S(1)}, u32[]{:S(2)}, u32[]{:S(2)}) collective-permute-start(bf16[144,768]{1,0:T(8,128)(2,1)S(1)} %get-tuple-element.30.refs_0_), channel_id=1, source_target_pairs={{0,16},{1,19},{4,20},{5,23},{8,24},{9,27},{12,28},{13,31},{32,48},... | collective-permute-start | bytes 663560 | tf_op jit(solution)/shard_map/ppermute | solution.py:37
  6.8 7.1 %collective-permute-start.3 = (bf16[144,768]{1,0:T(8,128)(2,1)S(1)}, bf16[144,768]{1,0:T(8,128)(2,1)S(1)}, u32[]{:S(2)}, u32[]{:S(2)}) collective-permute-start(bf16[144,768]{1,0:T(8,128)(2,1)S(1)} %get-tuple-element.31.refs_2_), channel_id=1, source_target_pairs={{0,32},{1,5},{4,36},{5,9},{8,40},{9,13},{12,44},{13,1},{32,64},{33... | collective-permute-start | bytes 663560 | tf_op jit(solution)/shard_map/ppermute | solution.py:37
  8.4 7.4 %collective-permute-start.2 = (bf16[144,768]{1,0:T(8,128)(2,1)S(1)}, bf16[144,768]{1,0:T(8,128)(2,1)S(1)}, u32[]{:S(2)}, u32[]{:S(2)}) collective-permute-start(bf16[144,768]{1,0:T(8,128)(2,1)S(1)} %get-tuple-element.31.refs_2_), channel_id=1, source_target_pairs={{0,96},{1,13},{4,100},{5,1},{8,104},{9,5},{12,108},{13,9},{32,0},{... | collective-permute-start | bytes 663560 | tf_op jit(solution)/shard_map/ppermute | solution.py:37
  10.5 6.9 %collective-permute-start.1 = (bf16[144,768]{1,0:T(8,128)(2,1)S(1)}, bf16[144,768]{1,0:T(8,128)(2,1)S(1)}, u32[]{:S(2)}, u32[]{:S(2)}) collective-permute-start(bf16[144,768]{1,0:T(8,128)(2,1)S(1)} %get-tuple-element.31.refs_2_), channel_id=1, source_target_pairs={{0,64},{1,9},{4,68},{5,13},{8,72},{9,1},{12,76},{13,5},{32,96},{33... | collective-permute-start | bytes 663560 | tf_op jit(solution)/shard_map/ppermute | solution.py:37
  17.5 11.5 %collective-permute-start.7 = (bf16[528,768]{1,0:T(8,128)(2,1)S(1)}, bf16[528,768]{1,0:T(8,128)(2,1)S(1)}, u32[]{:S(2)}, u32[]{:S(2)}) collective-permute-start(bf16[528,768]{1,0:T(8,128)(2,1)S(1)} %get-tuple-element.34.refs_4_), channel_id=1, source_target_pairs={{0,18},{1,17},{4,22},{5,21},{8,26},{9,25},{12,30},{13,29},{32,50},... | collective-permute-start | bytes 2433032 | tf_op jit(solution)/shard_map/ppermute | solution.py:37
  17.6 5.0 %collective-permute-start.8 = (bf16[272,768]{1,0:T(8,128)(2,1)S(1)}, bf16[272,768]{1,0:T(8,128)(2,1)S(1)}, u32[]{:S(2)}, u32[]{:S(2)}) collective-permute-start(bf16[272,768]{1,0:T(8,128)(2,1)S(1)} %get-tuple-element.33.refs_0_), channel_id=1, source_target_pairs={{0,1},{1,0},{4,5},{5,4},{8,9},{9,8},{12,13},{13,12},{32,33},{33,32... | collective-permute-start | bytes 1253384 | tf_op jit(solution)/shard_map/ppermute | solution.py:37
  19.5 11.4 %collective-permute-start.6 = (bf16[272,768]{1,0:T(8,128)(2,1)S(1)}, bf16[272,768]{1,0:T(8,128)(2,1)S(1)}, u32[]{:S(2)}, u32[]{:S(2)}) collective-permute-start(bf16[272,768]{1,0:T(8,128)(2,1)S(1)} %get-tuple-element.33.refs_0_), channel_id=1, source_target_pairs={{0,4},{1,33},{4,8},{5,37},{8,12},{9,41},{12,0},{13,45},{32,36},{33... | collective-permute-start | bytes 1253384 | tf_op jit(solution)/shard_map/ppermute | solution.py:37
  20.6 11.0 %collective-permute-start.5 = (bf16[272,768]{1,0:T(8,128)(2,1)S(1)}, bf16[272,768]{1,0:T(8,128)(2,1)S(1)}, u32[]{:S(2)}, u32[]{:S(2)}) collective-permute-start(bf16[272,768]{1,0:T(8,128)(2,1)S(1)} %get-tuple-element.33.refs_0_), channel_id=1, source_target_pairs={{0,12},{1,97},{4,0},{5,101},{8,4},{9,105},{12,8},{13,109},{32,44},... | collective-permute-start | bytes 1253384 | tf_op jit(solution)/shard_map/ppermute | solution.py:37
  22.1 11.4 %collective-permute-start.4 = (bf16[272,768]{1,0:T(8,128)(2,1)S(1)}, bf16[272,768]{1,0:T(8,128)(2,1)S(1)}, u32[]{:S(2)}, u32[]{:S(2)}) collective-permute-start(bf16[272,768]{1,0:T(8,128)(2,1)S(1)} %get-tuple-element.33.refs_0_), channel_id=1, source_target_pairs={{0,8},{1,65},{4,12},{5,69},{8,0},{9,73},{12,4},{13,77},{32,40},{33... | collective-permute-start | bytes 1253384 | tf_op jit(solution)/shard_map/ppermute | solution.py:37
  22.6 17.2 %collective-permute-start.12 = (bf16[528,768]{1,0:T(8,128)(2,1)S(1)}, bf16[528,768]{1,0:T(8,128)(2,1)S(1)}, u32[]{:S(2)}, u32[]{:S(2)}) collective-permute-start(bf16[528,768]{1,0:T(8,128)(2,1)S(1)} %get-tuple-element.34.refs_4_), channel_id=1, source_target_pairs={{0,1},{1,0},{4,5},{5,4},{8,9},{9,8},{12,13},{13,12},{32,33},{33,32... | collective-permute-start | bytes 2433032 | tf_op jit(solution)/shard_map/ppermute | solution.py:37
  28.9 13.6 %collective-permute-start.13 = (bf16[528,768]{1,0:T(8,128)(2,1)S(1)}, bf16[528,768]{1,0:T(8,128)(2,1)S(1)}, u32[]{:S(2)}, u32[]{:S(2)}) collective-permute-start(bf16[528,768]{1,0:T(8,128)(2,1)S(1)} %collective-permute-done.7.refs_5_), channel_id=1, source_target_pairs={{0,1},{1,0},{4,5},{5,4},{8,9},{9,8},{12,13},{13,12},{32,33},{33,32... | collective-permute-start | bytes 2433032 | tf_op jit(solution)/shard_map/ppermute | solution.py:37
  30.8 9.0 %collective-permute-start.11 = (bf16[272,768]{1,0:T(8,128)(2,1)S(1)}, bf16[272,768]{1,0:T(8,128)(2,1)S(1)}, u32[]{:S(2)}, u32[]{:S(2)}) collective-permute-start(bf16[272,768]{1,0:T(8,128)(2,1)S(1)} %collective-permute-done.6.refs_3_), channel_id=1, source_target_pairs={{0,1},{1,0},{4,5},{5,4},{8,9},{9,8},{12,13},{13,12},{32,33},{33,32... | collective-permute-start | bytes 1253384 | tf_op jit(solution)/shard_map/ppermute | solution.py:37
  31.6 8.2 %collective-permute-start.10 = (bf16[272,768]{1,0:T(8,128)(2,1)S(1)}, bf16[272,768]{1,0:T(8,128)(2,1)S(1)}, u32[]{:S(2)}, u32[]{:S(2)}) collective-permute-start(bf16[272,768]{1,0:T(8,128)(2,1)S(1)} %collective-permute-done.5.refs_2_), channel_id=1, source_target_pairs={{0,1},{1,0},{4,5},{5,4},{8,9},{9,8},{12,13},{13,12},{32,33},{33,32... | collective-permute-start | bytes 1253384 | tf_op jit(solution)/shard_map/ppermute | solution.py:37
  33.6 6.3 %collective-permute-start.9 = (bf16[272,768]{1,0:T(8,128)(2,1)S(1)}, bf16[272,768]{1,0:T(8,128)(2,1)S(1)}, u32[]{:S(2)}, u32[]{:S(2)}) collective-permute-start(bf16[272,768]{1,0:T(8,128)(2,1)S(1)} %collective-permute-done.4.refs_1_), channel_id=1, source_target_pairs={{0,1},{1,0},{4,5},{5,4},{8,9},{9,8},{12,13},{13,12},{32,33},{33,32... | collective-permute-start | bytes 1253384 | tf_op jit(solution)/shard_map/ppermute | solution.py:37
  42.5 7.4 %collective-permute-start.14 = (f32[512,768]{1,0:T(8,128)S(1)}, f32[512,768]{1,0:T(8,128)S(1)}, u32[]{:S(2)}, u32[]{:S(2)}) collective-permute-start(f32[512,768]{1,0:T(8,128)S(1)} %get-tuple-element.47), channel_id=1, source_target_pairs={{0,1},{1,0},{4,5},{5,4},{8,9},{9,8},{12,13},{13,12},{32,33},{33,32... | collective-permute-start | bytes 4718600 | tf_op jit(solution)/shard_map/ppermute | solution.py:37
  51.5 13.6 %collective-permute-start.16 = (f16[512,768]{1,0:T(8,128)(2,1)}, f16[512,768]{1,0:T(8,128)(2,1)S(1)}, u32[]{:S(2)}, u32[]{:S(2)}) collective-permute-start(f16[512,768]{1,0:T(8,128)(2,1)} %convert_element_type.43), channel_id=1, source_target_pairs={{0,18},{1,17},{4,22},{5,21},{8,26},{9,25},{12,30},{13,29},{32,50},... | collective-permute-start | bytes 2359304 | tf_op jit(solution)/shard_map/ppermute | solution.py:37
  53.0 13.5 %collective-permute-start.17 = (f16[256,768]{1,0:T(8,128)(2,1)}, f16[256,768]{1,0:T(8,128)(2,1)}, u32[]{:S(2)}, u32[]{:S(2)}) collective-permute-start(f16[256,768]{1,0:T(8,128)(2,1)} %get-tuple-element.59), channel_id=1, source_target_pairs={{0,8},{1,65},{4,12},{5,69},{8,0},{9,73},{12,4},{13,77},{32,40},{33... | collective-permute-start | bytes 1179656 | tf_op jit(solution)/shard_map/ppermute | solution.py:37
  54.7 11.9 %collective-permute-start.19 = (f16[256,768]{1,0:T(8,128)(2,1)}, f16[256,768]{1,0:T(8,128)(2,1)}, u32[]{:S(2)}, u32[]{:S(2)}) collective-permute-start(f16[256,768]{1,0:T(8,128)(2,1)} %get-tuple-element.60), channel_id=1, source_target_pairs={{0,12},{1,97},{4,0},{5,101},{8,4},{9,105},{12,8},{13,109},{32,44},... | collective-permute-start | bytes 1179656 | tf_op jit(solution)/shard_map/ppermute | solution.py:37
  56.6 10.0 %collective-permute-start.18 = (f16[256,768]{1,0:T(8,128)(2,1)}, f16[256,768]{1,0:T(8,128)(2,1)}, u32[]{:S(2)}, u32[]{:S(2)}) collective-permute-start(f16[256,768]{1,0:T(8,128)(2,1)} %get-tuple-element.61), channel_id=1, source_target_pairs={{0,4},{1,33},{4,8},{5,37},{8,12},{9,41},{12,0},{13,45},{32,36},{33... | collective-permute-start | bytes 1179656 | tf_op jit(solution)/shard_map/ppermute | solution.py:37
  56.6 24.6 %all-to-all-start = ((f32[128,1,128]{2,1,0:T(1,128)}), f32[128,1,128]{2,1,0:T(1,128)S(1)}, u32[]{:S(2)}, u32[]{:S(2)}) async-start(f32[128,1,128]{2,1,0:T(1,128)} %bitcast.2), calls=%async_computation | async-start | bytes 131072 | tf_op jit(solution)/shard_map/all_to_all | solution.py:427
  68.0 7.5 %collective-permute-start.20 = (f16[128,768]{1,0:T(8,128)(2,1)S(1)}, f16[128,768]{1,0:T(8,128)(2,1)S(1)}, u32[]{:S(2)}, u32[]{:S(2)}) collective-permute-start(f16[128,768]{1,0:T(8,128)(2,1)S(1)} %slice_convert_fusion), channel_id=1, source_target_pairs={{0,16},{1,19},{4,20},{5,23},{8,24},{9,27},{12,28},{13,31},{32,48},... | collective-permute-start | bytes 589832 | tf_op jit(solution)/shard_map/ppermute | solution.py:37
  70.8 6.3 %collective-permute-start.21 = (f16[128,768]{1,0:T(8,128)(2,1)S(1)}, f16[128,768]{1,0:T(8,128)(2,1)S(1)}, u32[]{:S(2)}, u32[]{:S(2)}) collective-permute-start(f16[128,768]{1,0:T(8,128)(2,1)S(1)} %get-tuple-element.62), channel_id=1, source_target_pairs={{0,64},{1,9},{4,68},{5,13},{8,72},{9,1},{12,76},{13,5},{32,96},{33... | collective-permute-start | bytes 589832 | tf_op jit(solution)/shard_map/ppermute | solution.py:37
  74.0 6.0 %collective-permute-start.23 = (f16[128,768]{1,0:T(8,128)(2,1)S(1)}, f16[128,768]{1,0:T(8,128)(2,1)S(1)}, u32[]{:S(2)}, u32[]{:S(2)}) collective-permute-start(f16[128,768]{1,0:T(8,128)(2,1)S(1)} %get-tuple-element.63), channel_id=1, source_target_pairs={{0,96},{1,13},{4,100},{5,1},{8,104},{9,5},{12,108},{13,9},{32,0},{... | collective-permute-start | bytes 589832 | tf_op jit(solution)/shard_map/ppermute | solution.py:37
  74.6 6.0 %collective-permute-start.22 = (f16[128,768]{1,0:T(8,128)(2,1)S(1)}, f16[128,768]{1,0:T(8,128)(2,1)S(1)}, u32[]{:S(2)}, u32[]{:S(2)}) collective-permute-start(f16[128,768]{1,0:T(8,128)(2,1)S(1)} %get-tuple-element.64), channel_id=1, source_target_pairs={{0,32},{1,5},{4,36},{5,9},{8,40},{9,13},{12,44},{13,1},{32,64},{33... | collective-permute-start | bytes 589832 | tf_op jit(solution)/shard_map/ppermute | solution.py:37
  (7 other events, 30.5 us)

commit v3 on v2

--- a/solution.py
+++ b/solution.py
@@ -421,7 +421,7 @@
         24 * tall * width,
     )
     column_sum = column_keep + send(column_send.astype(SEND), column_move).astype(F32)
-    pair_sum = pair_keep + 0.0 * column_sum[0, 0]
+    pair_sum = pair_keep + 0.0 * column_sum[:span]
     for index, step in enumerate(STEPS):
         pair_sum = pair_sum + send(pair_send[index].astype(SEND), pair_step(-step)).astype(F32)
     all_sums = lax.all_to_all(sums, AXES, 0, 0, tiled=True)

time: 82.7 us -> 81.6 us (0.987)
  transfers between devices with their start and end apart: 25 -> 25, of which waited for: 8 -> 9; matrix products, arithmetic and copies ran while one was open for 4% -> 4% of each run, Pallas kernels for 17% -> 17%
where the time goes in v3:
time: 81.6 us; the launch traced here: 81.3 us
  starting transfers between devices  41.8 us (51%)
  Pallas kernels  16.1 us (20%)
  waiting for transfers between devices  14.3 us (18%)
  local copies, waits for them, and re-layouts  3.69 us (5%)
  other arithmetic  3.09 us (4%)
  between operations  2.31 us (3%)
    ppermute x24, starting transfers between devices, send(): return lax.ppermute(values, AXES, pairs(move))  33.3 us
    pallas_call x9, Pallas kernels, call(): pl.pallas_call(kernel, out_shape=[jax.ShapeDtypeStruct(shape, kind) for s...  16.1 us
    ppermute x24, waiting for transfers between devices, send(): return lax.ppermute(values, AXES, pairs(move))  14.3 us
    all_to_all x1, starting transfers between devices, body(): all_sums = lax.all_to_all(sums, AXES, 0, 0, tiled=True)  8.5 us
    unnamed x12, local copies, waits for them, and re-layouts  2.52 us
  transfers between devices with their start and end apart: 25, of which 9 were waited for; matrix products, arithmetic and copies ran while one was open for 4% of the time, Pallas kernels for 17%

profile of v3, /device:TPU:1, one launch (start us, length us, event | category | flops | bytes accessed | tf_op | source)
XLA Modules:
  0.0 81.3 jit_solution(6693786528810251112)
XLA Ops:
  3.4 3.4 %collective-permute-start = (bf16[144,768]{1,0:T(8,128)(2,1)S(1)}, bf16[144,768]{1,0:T(8,128)(2,1)S(1)}, u32[]{:S(2)}, u32[]{:S(2)}) collective-permute-start(bf16[144,768]{1,0:T(8,128)(2,1)S(1)} %get-tuple-element.30.refs_0_), channel_id=1, source_target_pairs={{0,16},{1,19},{4,20},{5,23},{8,24},{9,27},{12,28},{13,31},{32,48},... | collective-permute-start | bytes 663560 | tf_op jit(solution)/shard_map/ppermute | solution.py:37
  6.8 1.6 %collective-permute-start.3 = (bf16[144,768]{1,0:T(8,128)(2,1)S(1)}, bf16[144,768]{1,0:T(8,128)(2,1)S(1)}, u32[]{:S(2)}, u32[]{:S(2)}) collective-permute-start(bf16[144,768]{1,0:T(8,128)(2,1)S(1)} %get-tuple-element.31.refs_2_), channel_id=1, source_target_pairs={{0,32},{1,5},{4,36},{5,9},{8,40},{9,13},{12,44},{13,1},{32,64},{33... | collective-permute-start | bytes 663560 | tf_op jit(solution)/shard_map/ppermute | solution.py:37
  8.4 2.1 %collective-permute-start.2 = (bf16[144,768]{1,0:T(8,128)(2,1)S(1)}, bf16[144,768]{1,0:T(8,128)(2,1)S(1)}, u32[]{:S(2)}, u32[]{:S(2)}) collective-permute-start(bf16[144,768]{1,0:T(8,128)(2,1)S(1)} %get-tuple-element.31.refs_2_), channel_id=1, source_target_pairs={{0,96},{1,13},{4,100},{5,1},{8,104},{9,5},{12,108},{13,9},{32,0},{... | collective-permute-start | bytes 663560 | tf_op jit(solution)/shard_map/ppermute | solution.py:37
  13.8 1.9 %collective-permute-done.2.refs_4_ = bf16[144,768]{1,0:T(8,128)(2,1)S(1)} collective-permute-done((bf16[144,768]{1,0:T(8,128)(2,1)S(1)}, bf16[144,768]{1,0:T(8,128)(2,1)S(1)}, u32[]{:S(2)}, u32[]{:S(2)}) %collective-permute-start.2) | collective-permute-done | bytes 221216 | tf_op jit(solution)/shard_map/ppermute | solution.py:37
  15.8 1.6 %collective-permute-done.1.refs_3_ = bf16[144,768]{1,0:T(8,128)(2,1)S(1)} collective-permute-done((bf16[144,768]{1,0:T(8,128)(2,1)S(1)}, bf16[144,768]{1,0:T(8,128)(2,1)S(1)}, u32[]{:S(2)}, u32[]{:S(2)}) %collective-permute-start.1) | collective-permute-done | bytes 221216 | tf_op jit(solution)/shard_map/ppermute | solution.py:37
  17.6 1.9 %collective-permute-start.8 = (bf16[272,768]{1,0:T(8,128)(2,1)S(1)}, bf16[272,768]{1,0:T(8,128)(2,1)S(1)}, u32[]{:S(2)}, u32[]{:S(2)}) collective-permute-start(bf16[272,768]{1,0:T(8,128)(2,1)S(1)} %get-tuple-element.33.refs_0_), channel_id=1, source_target_pairs={{0,1},{1,0},{4,5},{5,4},{8,9},{9,8},{12,13},{13,12},{32,33},{33,32... | collective-permute-start | bytes 1253384 | tf_op jit(solution)/shard_map/ppermute | solution.py:37
  20.6 1.5 %collective-permute-start.5 = (bf16[272,768]{1,0:T(8,128)(2,1)S(1)}, bf16[272,768]{1,0:T(8,128)(2,1)S(1)}, u32[]{:S(2)}, u32[]{:S(2)}) collective-permute-start(bf16[272,768]{1,0:T(8,128)(2,1)S(1)} %get-tuple-element.33.refs_0_), channel_id=1, source_target_pairs={{0,12},{1,97},{4,0},{5,101},{8,4},{9,105},{12,8},{13,109},{32,44},... | collective-permute-start | bytes 1253384 | tf_op jit(solution)/shard_map/ppermute | solution.py:37
  22.6 2.8 %collective-permute-start.12 = (bf16[528,768]{1,0:T(8,128)(2,1)S(1)}, bf16[528,768]{1,0:T(8,128)(2,1)S(1)}, u32[]{:S(2)}, u32[]{:S(2)}) collective-permute-start(bf16[528,768]{1,0:T(8,128)(2,1)S(1)} %get-tuple-element.34.refs_4_), channel_id=1, source_target_pairs={{0,1},{1,0},{4,5},{5,4},{8,9},{9,8},{12,13},{13,12},{32,33},{33,32... | collective-permute-start | bytes 2433032 | tf_op jit(solution)/shard_map/ppermute | solution.py:37
  25.4 3.6 %collective-permute-done.7.refs_5_ = bf16[528,768]{1,0:T(8,128)(2,1)S(1)} collective-permute-done((bf16[528,768]{1,0:T(8,128)(2,1)S(1)}, bf16[528,768]{1,0:T(8,128)(2,1)S(1)}, u32[]{:S(2)}, u32[]{:S(2)}) %collective-permute-start.7) | collective-permute-done | bytes 811040 | tf_op jit(solution)/shard_map/ppermute | solution.py:37
  28.9 1.9 %collective-permute-start.13 = (bf16[528,768]{1,0:T(8,128)(2,1)S(1)}, bf16[528,768]{1,0:T(8,128)(2,1)S(1)}, u32[]{:S(2)}, u32[]{:S(2)}) collective-permute-start(bf16[528,768]{1,0:T(8,128)(2,1)S(1)} %collective-permute-done.7.refs_5_), channel_id=1, source_target_pairs={{0,1},{1,0},{4,5},{5,4},{8,9},{9,8},{12,13},{13,12},{32,33},{33,32... | collective-permute-start | bytes 2433032 | tf_op jit(solution)/shard_map/ppermute | solution.py:37
  31.6 2.0 %collective-permute-start.10 = (bf16[272,768]{1,0:T(8,128)(2,1)S(1)}, bf16[272,768]{1,0:T(8,128)(2,1)S(1)}, u32[]{:S(2)}, u32[]{:S(2)}) collective-permute-start(bf16[272,768]{1,0:T(8,128)(2,1)S(1)} %collective-permute-done.5.refs_2_), channel_id=1, source_target_pairs={{0,1},{1,0},{4,5},{5,4},{8,9},{9,8},{12,13},{13,12},{32,33},{33,32... | collective-permute-start | bytes 1253384 | tf_op jit(solution)/shard_map/ppermute | solution.py:37
  33.6 1.9 %collective-permute-start.9 = (bf16[272,768]{1,0:T(8,128)(2,1)S(1)}, bf16[272,768]{1,0:T(8,128)(2,1)S(1)}, u32[]{:S(2)}, u32[]{:S(2)}) collective-permute-start(bf16[272,768]{1,0:T(8,128)(2,1)S(1)} %collective-permute-done.4.refs_1_), channel_id=1, source_target_pairs={{0,1},{1,0},{4,5},{5,4},{8,9},{9,8},{12,13},{13,12},{32,33},{33,32... | collective-permute-start | bytes 1253384 | tf_op jit(solution)/shard_map/ppermute | solution.py:37
  35.5 4.3 %shard_map.78 = (f32[1024,768]{1,0:T(8,128)S(1)}, bf16[2048,1024]{1,0:T(8,128)(2,1)S(1)}, bf16[2048,768]{1,0:T(8,128)(2,1)S(1)}, f32[3,8,128]{2,1,0:T(8,128)S(1)}, bf16[1024,768]{1,0:T(8,128)(2,1)S(1)}) custom-call(f32[8,128]{1,0:T(8,128)S(1)} %get-tuple-element.32.given, bf16[272,768]{1,0:T(8,128)(2,1)S(1)} %get-tuple-element.33.refs_0_, ...), custom_call_target="tpu_custom_call" | custom-call | flops 3221225472 | bytes 12582912 | tf_op jit(solution)/shard_map/pallas_call | solution.py:327
  39.8 2.6 %shard_map.79 = (f32[512,768]{1,0:T(8,128)S(1)}, bf16[2048,1024]{1,0:T(8,128)(2,1)S(1)}, bf16[2048,768]{1,0:T(8,128)(2,1)S(1)}, f32[3,8,128]{2,1,0:T(8,128)S(1)}) custom-call(f32[8,128]{1,0:T(8,128)S(1)} %get-tuple-element.32.given, bf16[272,768]{1,0:T(8,128)(2,1)S(1)} %collective-permute-done.8.refs_0_, ...), custom_call_target="tpu_custom_call", output_to_operand_aliasing={{1}: (7, {}), {2}: (8, {})} | custom-call | flops 1610612736 | bytes 6291456 | tf_op jit(solution)/shard_map/pallas_call | solution.py:327
  42.6 2.8 %shard_map.80 = (f32[512,768]{1,0:T(8,128)S(1)}, bf16[2048,1024]{1,0:T(8,128)(2,1)S(1)}, bf16[2048,768]{1,0:T(8,128)(2,1)S(1)}, f32[3,8,128]{2,1,0:T(8,128)S(1)}) custom-call(f32[8,128]{1,0:T(8,128)S(1)} %get-tuple-element.32.given, bf16[272,768]{1,0:T(8,128)(2,1)S(1)} %collective-permute-done.8.refs_0_, ...), custom_call_target="tpu_custom_call", output_to_operand_aliasing={{1}: (7, {}), {2}: (8, {})} | custom-call | flops 1610612736 | bytes 6291456 | tf_op jit(solution)/shard_map/pallas_call | solution.py:327
  45.9 4.0 %shard_map.81 = (f32[512,768]{1,0:T(8,128)S(1)}, f32[512,768]{1,0:T(8,128)S(1)}, f32[128,128]{1,0:T(8,128)}) custom-call(f32[3,8,128]{2,1,0:T(8,128)S(1)} %get-tuple-element.35.refs_0_, f32[3,8,128]{2,1,0:T(8,128)S(1)} %get-tuple-element.39.refs_1_, f32[3,8,128]{2,1,0:T(8,128)S(1)} %get-tuple-element.42.refs_2_, bf16[1,128]{1,0:T(2,128)(2,1)S(1)} %bitcast.13, ...), custom_call_target="tpu_custom_call" | custom-call | flops 3221225472 | bytes 9437184 | tf_op jit(solution)/shard_map/pallas_call | solution.py:327
  53.0 1.6 %collective-permute-start.17 = (f16[256,768]{1,0:T(8,128)(2,1)}, f16[256,768]{1,0:T(8,128)(2,1)}, u32[]{:S(2)}, u32[]{:S(2)}) collective-permute-start(f16[256,768]{1,0:T(8,128)(2,1)} %get-tuple-element.59), channel_id=1, source_target_pairs={{0,8},{1,65},{4,12},{5,69},{8,0},{9,73},{12,4},{13,77},{32,40},{33... | collective-permute-start | bytes 1179656 | tf_op jit(solution)/shard_map/ppermute | solution.py:37
  54.7 1.9 %collective-permute-start.19 = (f16[256,768]{1,0:T(8,128)(2,1)}, f16[256,768]{1,0:T(8,128)(2,1)}, u32[]{:S(2)}, u32[]{:S(2)}) collective-permute-start(f16[256,768]{1,0:T(8,128)(2,1)} %get-tuple-element.60), channel_id=1, source_target_pairs={{0,12},{1,97},{4,0},{5,101},{8,4},{9,105},{12,8},{13,109},{32,44},... | collective-permute-start | bytes 1179656 | tf_op jit(solution)/shard_map/ppermute | solution.py:37
  56.6 8.5 %all-to-all-start = ((f32[128,1,128]{2,1,0:T(1,128)}), f32[128,1,128]{2,1,0:T(1,128)S(1)}, u32[]{:S(2)}, u32[]{:S(2)}) async-start(f32[128,1,128]{2,1,0:T(1,128)} %bitcast.2), calls=%async_computation | async-start | bytes 131072 | tf_op jit(solution)/shard_map/all_to_all | solution.py:427
  66.0 1.5 %fusion.3 = f32[256,768]{1,0:T(8,128)S(1)} fusion(f32[256,768]{1,0:T(8,128)S(1)} %get-tuple-element.51, f32[512,768]{1,0:T(8,128)S(1)} %get-tuple-element.58, f16[256,768]{1,0:T(8,128)(2,1)} %collective-permute-done.19, f16[256,768]{1,0:T(8,128)(2,1)} %collective-permute-done.18, f16[256,768]{1,0:T(8,128)(2,1)} %collective-permute-done.17), kind=kLoop, calls=%fused_computation.5 | loop fusion | flops 1572864 | bytes 3538944 | tf_op jit(solution)/shard_map/add | solution.py:426
  67.5 2.1 %collective-permute-start.20 = (f16[128,768]{1,0:T(8,128)(2,1)S(1)}, f16[128,768]{1,0:T(8,128)(2,1)S(1)}, u32[]{:S(2)}, u32[]{:S(2)}) collective-permute-start(f16[128,768]{1,0:T(8,128)(2,1)S(1)} %slice_convert_fusion), channel_id=1, source_target_pairs={{0,16},{1,19},{4,20},{5,23},{8,24},{9,27},{12,28},{13,31},{32,48},... | collective-permute-start | bytes 589832 | tf_op jit(solution)/shard_map/ppermute | solution.py:37
  69.7 3.2 %collective-permute-start.21 = (f16[128,768]{1,0:T(8,128)(2,1)S(1)}, f16[128,768]{1,0:T(8,128)(2,1)S(1)}, u32[]{:S(2)}, u32[]{:S(2)}) collective-permute-start(f16[128,768]{1,0:T(8,128)(2,1)S(1)} %get-tuple-element.62), channel_id=1, source_target_pairs={{0,64},{1,9},{4,68},{5,13},{8,72},{9,1},{12,76},{13,5},{32,96},{33... | collective-permute-start | bytes 589832 | tf_op jit(solution)/shard_map/ppermute | solution.py:37
  74.4 1.9 %collective-permute-done.21 = f16[128,768]{1,0:T(8,128)(2,1)S(1)} collective-permute-done((f16[128,768]{1,0:T(8,128)(2,1)S(1)}, f16[128,768]{1,0:T(8,128)(2,1)S(1)}, u32[]{:S(2)}, u32[]{:S(2)}) %collective-permute-start.21) | collective-permute-done | bytes 196640 | tf_op jit(solution)/shard_map/ppermute | solution.py:37
  76.3 2.6 %collective-permute-done.23 = f16[128,768]{1,0:T(8,128)(2,1)S(1)} collective-permute-done((f16[128,768]{1,0:T(8,128)(2,1)S(1)}, f16[128,768]{1,0:T(8,128)(2,1)S(1)}, u32[]{:S(2)}, u32[]{:S(2)}) %collective-permute-start.23) | collective-permute-done | bytes 196640 | tf_op jit(solution)/shard_map/ppermute | solution.py:37
  (56 shorter events, 15.7 us)
Async XLA Ops:
  3.4 9.8 %collective-permute-start = (bf16[144,768]{1,0:T(8,128)(2,1)S(1)}, bf16[144,768]{1,0:T(8,128)(2,1)S(1)}, u32[]{:S(2)}, u32[]{:S(2)}) collective-permute-start(bf16[144,768]{1,0:T(8,128)(2,1)S(1)} %get-tuple-element.30.refs_0_), channel_id=1, source_target_pairs={{0,16},{1,19},{4,20},{5,23},{8,24},{9,27},{12,28},{13,31},{32,48},... | collective-permute-start | bytes 663560 | tf_op jit(solution)/shard_map/ppermute | solution.py:37
  6.8 7.1 %collective-permute-start.3 = (bf16[144,768]{1,0:T(8,128)(2,1)S(1)}, bf16[144,768]{1,0:T(8,128)(2,1)S(1)}, u32[]{:S(2)}, u32[]{:S(2)}) collective-permute-start(bf16[144,768]{1,0:T(8,128)(2,1)S(1)} %get-tuple-element.31.refs_2_), channel_id=1, source_target_pairs={{0,32},{1,5},{4,36},{5,9},{8,40},{9,13},{12,44},{13,1},{32,64},{33... | collective-permute-start | bytes 663560 | tf_op jit(solution)/shard_map/ppermute | solution.py:37
  8.4 7.4 %collective-permute-start.2 = (bf16[144,768]{1,0:T(8,128)(2,1)S(1)}, bf16[144,768]{1,0:T(8,128)(2,1)S(1)}, u32[]{:S(2)}, u32[]{:S(2)}) collective-permute-start(bf16[144,768]{1,0:T(8,128)(2,1)S(1)} %get-tuple-element.31.refs_2_), channel_id=1, source_target_pairs={{0,96},{1,13},{4,100},{5,1},{8,104},{9,5},{12,108},{13,9},{32,0},{... | collective-permute-start | bytes 663560 | tf_op jit(solution)/shard_map/ppermute | solution.py:37
  10.5 6.9 %collective-permute-start.1 = (bf16[144,768]{1,0:T(8,128)(2,1)S(1)}, bf16[144,768]{1,0:T(8,128)(2,1)S(1)}, u32[]{:S(2)}, u32[]{:S(2)}) collective-permute-start(bf16[144,768]{1,0:T(8,128)(2,1)S(1)} %get-tuple-element.31.refs_2_), channel_id=1, source_target_pairs={{0,64},{1,9},{4,68},{5,13},{8,72},{9,1},{12,76},{13,5},{32,96},{33... | collective-permute-start | bytes 663560 | tf_op jit(solution)/shard_map/ppermute | solution.py:37
  17.5 11.5 %collective-permute-start.7 = (bf16[528,768]{1,0:T(8,128)(2,1)S(1)}, bf16[528,768]{1,0:T(8,128)(2,1)S(1)}, u32[]{:S(2)}, u32[]{:S(2)}) collective-permute-start(bf16[528,768]{1,0:T(8,128)(2,1)S(1)} %get-tuple-element.34.refs_4_), channel_id=1, source_target_pairs={{0,18},{1,17},{4,22},{5,21},{8,26},{9,25},{12,30},{13,29},{32,50},... | collective-permute-start | bytes 2433032 | tf_op jit(solution)/shard_map/ppermute | solution.py:37
  17.6 5.0 %collective-permute-start.8 = (bf16[272,768]{1,0:T(8,128)(2,1)S(1)}, bf16[272,768]{1,0:T(8,128)(2,1)S(1)}, u32[]{:S(2)}, u32[]{:S(2)}) collective-permute-start(bf16[272,768]{1,0:T(8,128)(2,1)S(1)} %get-tuple-element.33.refs_0_), channel_id=1, source_target_pairs={{0,1},{1,0},{4,5},{5,4},{8,9},{9,8},{12,13},{13,12},{32,33},{33,32... | collective-permute-start | bytes 1253384 | tf_op jit(solution)/shard_map/ppermute | solution.py:37
  19.5 11.4 %collective-permute-start.6 = (bf16[272,768]{1,0:T(8,128)(2,1)S(1)}, bf16[272,768]{1,0:T(8,128)(2,1)S(1)}, u32[]{:S(2)}, u32[]{:S(2)}) collective-permute-start(bf16[272,768]{1,0:T(8,128)(2,1)S(1)} %get-tuple-element.33.refs_0_), channel_id=1, source_target_pairs={{0,4},{1,33},{4,8},{5,37},{8,12},{9,41},{12,0},{13,45},{32,36},{33... | collective-permute-start | bytes 1253384 | tf_op jit(solution)/shard_map/ppermute | solution.py:37
  20.6 11.0 %collective-permute-start.5 = (bf16[272,768]{1,0:T(8,128)(2,1)S(1)}, bf16[272,768]{1,0:T(8,128)(2,1)S(1)}, u32[]{:S(2)}, u32[]{:S(2)}) collective-permute-start(bf16[272,768]{1,0:T(8,128)(2,1)S(1)} %get-tuple-element.33.refs_0_), channel_id=1, source_target_pairs={{0,12},{1,97},{4,0},{5,101},{8,4},{9,105},{12,8},{13,109},{32,44},... | collective-permute-start | bytes 1253384 | tf_op jit(solution)/shard_map/ppermute | solution.py:37
  22.1 11.4 %collective-permute-start.4 = (bf16[272,768]{1,0:T(8,128)(2,1)S(1)}, bf16[272,768]{1,0:T(8,128)(2,1)S(1)}, u32[]{:S(2)}, u32[]{:S(2)}) collective-permute-start(bf16[272,768]{1,0:T(8,128)(2,1)S(1)} %get-tuple-element.33.refs_0_), channel_id=1, source_target_pairs={{0,8},{1,65},{4,12},{5,69},{8,0},{9,73},{12,4},{13,77},{32,40},{33... | collective-permute-start | bytes 1253384 | tf_op jit(solution)/shard_map/ppermute | solution.py:37
  22.6 17.2 %collective-permute-start.12 = (bf16[528,768]{1,0:T(8,128)(2,1)S(1)}, bf16[528,768]{1,0:T(8,128)(2,1)S(1)}, u32[]{:S(2)}, u32[]{:S(2)}) collective-permute-start(bf16[528,768]{1,0:T(8,128)(2,1)S(1)} %get-tuple-element.34.refs_4_), channel_id=1, source_target_pairs={{0,1},{1,0},{4,5},{5,4},{8,9},{9,8},{12,13},{13,12},{32,33},{33,32... | collective-permute-start | bytes 2433032 | tf_op jit(solution)/shard_map/ppermute | solution.py:37
  28.9 13.6 %collective-permute-start.13 = (bf16[528,768]{1,0:T(8,128)(2,1)S(1)}, bf16[528,768]{1,0:T(8,128)(2,1)S(1)}, u32[]{:S(2)}, u32[]{:S(2)}) collective-permute-start(bf16[528,768]{1,0:T(8,128)(2,1)S(1)} %collective-permute-done.7.refs_5_), channel_id=1, source_target_pairs={{0,1},{1,0},{4,5},{5,4},{8,9},{9,8},{12,13},{13,12},{32,33},{33,32... | collective-permute-start | bytes 2433032 | tf_op jit(solution)/shard_map/ppermute | solution.py:37
  30.8 9.0 %collective-permute-start.11 = (bf16[272,768]{1,0:T(8,128)(2,1)S(1)}, bf16[272,768]{1,0:T(8,128)(2,1)S(1)}, u32[]{:S(2)}, u32[]{:S(2)}) collective-permute-start(bf16[272,768]{1,0:T(8,128)(2,1)S(1)} %collective-permute-done.6.refs_3_), channel_id=1, source_target_pairs={{0,1},{1,0},{4,5},{5,4},{8,9},{9,8},{12,13},{13,12},{32,33},{33,32... | collective-permute-start | bytes 1253384 | tf_op jit(solution)/shard_map/ppermute | solution.py:37
  31.6 8.2 %collective-permute-start.10 = (bf16[272,768]{1,0:T(8,128)(2,1)S(1)}, bf16[272,768]{1,0:T(8,128)(2,1)S(1)}, u32[]{:S(2)}, u32[]{:S(2)}) collective-permute-start(bf16[272,768]{1,0:T(8,128)(2,1)S(1)} %collective-permute-done.5.refs_2_), channel_id=1, source_target_pairs={{0,1},{1,0},{4,5},{5,4},{8,9},{9,8},{12,13},{13,12},{32,33},{33,32... | collective-permute-start | bytes 1253384 | tf_op jit(solution)/shard_map/ppermute | solution.py:37
  33.6 6.3 %collective-permute-start.9 = (bf16[272,768]{1,0:T(8,128)(2,1)S(1)}, bf16[272,768]{1,0:T(8,128)(2,1)S(1)}, u32[]{:S(2)}, u32[]{:S(2)}) collective-permute-start(bf16[272,768]{1,0:T(8,128)(2,1)S(1)} %collective-permute-done.4.refs_1_), channel_id=1, source_target_pairs={{0,1},{1,0},{4,5},{5,4},{8,9},{9,8},{12,13},{13,12},{32,33},{33,32... | collective-permute-start | bytes 1253384 | tf_op jit(solution)/shard_map/ppermute | solution.py:37
  42.5 7.4 %collective-permute-start.14 = (f32[512,768]{1,0:T(8,128)S(1)}, f32[512,768]{1,0:T(8,128)S(1)}, u32[]{:S(2)}, u32[]{:S(2)}) collective-permute-start(f32[512,768]{1,0:T(8,128)S(1)} %get-tuple-element.47), channel_id=1, source_target_pairs={{0,1},{1,0},{4,5},{5,4},{8,9},{9,8},{12,13},{13,12},{32,33},{33,32... | collective-permute-start | bytes 4718600 | tf_op jit(solution)/shard_map/ppermute | solution.py:37
  51.5 13.6 %collective-permute-start.16 = (f16[512,768]{1,0:T(8,128)(2,1)}, f16[512,768]{1,0:T(8,128)(2,1)S(1)}, u32[]{:S(2)}, u32[]{:S(2)}) collective-permute-start(f16[512,768]{1,0:T(8,128)(2,1)} %convert_element_type.43), channel_id=1, source_target_pairs={{0,18},{1,17},{4,22},{5,21},{8,26},{9,25},{12,30},{13,29},{32,50},... | collective-permute-start | bytes 2359304 | tf_op jit(solution)/shard_map/ppermute | solution.py:37
  53.0 12.3 %collective-permute-start.17 = (f16[256,768]{1,0:T(8,128)(2,1)}, f16[256,768]{1,0:T(8,128)(2,1)}, u32[]{:S(2)}, u32[]{:S(2)}) collective-permute-start(f16[256,768]{1,0:T(8,128)(2,1)} %get-tuple-element.59), channel_id=1, source_target_pairs={{0,8},{1,65},{4,12},{5,69},{8,0},{9,73},{12,4},{13,77},{32,40},{33... | collective-permute-start | bytes 1179656 | tf_op jit(solution)/shard_map/ppermute | solution.py:37
  54.7 10.7 %collective-permute-start.19 = (f16[256,768]{1,0:T(8,128)(2,1)}, f16[256,768]{1,0:T(8,128)(2,1)}, u32[]{:S(2)}, u32[]{:S(2)}) collective-permute-start(f16[256,768]{1,0:T(8,128)(2,1)} %get-tuple-element.60), channel_id=1, source_target_pairs={{0,12},{1,97},{4,0},{5,101},{8,4},{9,105},{12,8},{13,109},{32,44},... | collective-permute-start | bytes 1179656 | tf_op jit(solution)/shard_map/ppermute | solution.py:37
  56.6 9.4 %collective-permute-start.18 = (f16[256,768]{1,0:T(8,128)(2,1)}, f16[256,768]{1,0:T(8,128)(2,1)}, u32[]{:S(2)}, u32[]{:S(2)}) collective-permute-start(f16[256,768]{1,0:T(8,128)(2,1)} %get-tuple-element.61), channel_id=1, source_target_pairs={{0,4},{1,33},{4,8},{5,37},{8,12},{9,41},{12,0},{13,45},{32,36},{33... | collective-permute-start | bytes 1179656 | tf_op jit(solution)/shard_map/ppermute | solution.py:37
  56.6 23.5 %all-to-all-start = ((f32[128,1,128]{2,1,0:T(1,128)}), f32[128,1,128]{2,1,0:T(1,128)S(1)}, u32[]{:S(2)}, u32[]{:S(2)}) async-start(f32[128,1,128]{2,1,0:T(1,128)} %bitcast.2), calls=%async_computation | async-start | bytes 131072 | tf_op jit(solution)/shard_map/all_to_all | solution.py:427
  67.5 6.9 %collective-permute-start.20 = (f16[128,768]{1,0:T(8,128)(2,1)S(1)}, f16[128,768]{1,0:T(8,128)(2,1)S(1)}, u32[]{:S(2)}, u32[]{:S(2)}) collective-permute-start(f16[128,768]{1,0:T(8,128)(2,1)S(1)} %slice_convert_fusion), channel_id=1, source_target_pairs={{0,16},{1,19},{4,20},{5,23},{8,24},{9,27},{12,28},{13,31},{32,48},... | collective-permute-start | bytes 589832 | tf_op jit(solution)/shard_map/ppermute | solution.py:37
  69.7 6.6 %collective-permute-start.21 = (f16[128,768]{1,0:T(8,128)(2,1)S(1)}, f16[128,768]{1,0:T(8,128)(2,1)S(1)}, u32[]{:S(2)}, u32[]{:S(2)}) collective-permute-start(f16[128,768]{1,0:T(8,128)(2,1)S(1)} %get-tuple-element.62), channel_id=1, source_target_pairs={{0,64},{1,9},{4,68},{5,13},{8,72},{9,1},{12,76},{13,5},{32,96},{33... | collective-permute-start | bytes 589832 | tf_op jit(solution)/shard_map/ppermute | solution.py:37
  72.9 6.0 %collective-permute-start.23 = (f16[128,768]{1,0:T(8,128)(2,1)S(1)}, f16[128,768]{1,0:T(8,128)(2,1)S(1)}, u32[]{:S(2)}, u32[]{:S(2)}) collective-permute-start(f16[128,768]{1,0:T(8,128)(2,1)S(1)} %get-tuple-element.63), channel_id=1, source_target_pairs={{0,96},{1,13},{4,100},{5,1},{8,104},{9,5},{12,108},{13,9},{32,0},{... | collective-permute-start | bytes 589832 | tf_op jit(solution)/shard_map/ppermute | solution.py:37
  73.5 6.0 %collective-permute-start.22 = (f16[128,768]{1,0:T(8,128)(2,1)S(1)}, f16[128,768]{1,0:T(8,128)(2,1)S(1)}, u32[]{:S(2)}, u32[]{:S(2)}) collective-permute-start(f16[128,768]{1,0:T(8,128)(2,1)S(1)} %get-tuple-element.64), channel_id=1, source_target_pairs={{0,32},{1,5},{4,36},{5,9},{8,40},{9,13},{12,44},{13,1},{32,64},{33... | collective-permute-start | bytes 589832 | tf_op jit(solution)/shard_map/ppermute | solution.py:37
  (7 other events, 30.6 us)

commit v4 on v3

--- a/solution.py
+++ b/solution.py
@@ -61,7 +61,7 @@
     )
 
 
-STEPS = (2, 3, 1)
+STEPS = (3, 2, 1)
 
 
 def on_core():

time: 81.6 us -> 82 us (level)
  starting transfers between devices: 41.8 us -> 43 us
    ppermute x24, starting transfers between devices: 33.3 us -> 34.3 us  [send(): return lax.ppermute(values, AXES, pairs(move))]
  transfers between devices with their start and end apart: 25 -> 25, of which waited for: 9 -> 8; matrix products, arithmetic and copies ran while one was open for 4% -> 4% of each run, Pallas kernels for 17% -> 17%
where the time goes in v4:
time: 82 us; the launch traced here: 81.8 us
  starting transfers between devices  43 us (52%)
  Pallas kernels  16.1 us (20%)
  waiting for transfers between devices  13.6 us (17%)
  local copies, waits for them, and re-layouts  3.69 us (4%)
  other arithmetic  3.09 us (4%)
  between operations  2.29 us (3%)
    ppermute x24, starting transfers between devices, send(): return lax.ppermute(values, AXES, pairs(move))  34.3 us
    pallas_call x9, Pallas kernels, call(): pl.pallas_call(kernel, out_shape=[jax.ShapeDtypeStruct(shape, kind) for s...  16.1 us
    ppermute x24, waiting for transfers between devices, send(): return lax.ppermute(values, AXES, pairs(move))  13.6 us
    all_to_all x1, starting transfers between devices, body(): all_sums = lax.all_to_all(sums, AXES, 0, 0, tiled=True)  8.7 us
    unnamed x12, local copies, waits for them, and re-layouts  2.51 us
  transfers between devices with their start and end apart: 25, of which 8 were waited for; matrix products, arithmetic and copies ran while one was open for 4% of the time, Pallas kernels for 17%

profile of v4, /device:TPU:1, one launch (start us, length us, event | category | flops | bytes accessed | tf_op | source)
XLA Modules:
  0.0 81.8 jit_solution(14585398532641070918)
XLA Ops:
  3.4 3.4 %collective-permute-start = (bf16[144,768]{1,0:T(8,128)(2,1)S(1)}, bf16[144,768]{1,0:T(8,128)(2,1)S(1)}, u32[]{:S(2)}, u32[]{:S(2)}) collective-permute-start(bf16[144,768]{1,0:T(8,128)(2,1)S(1)} %get-tuple-element.30.refs_0_), channel_id=1, source_target_pairs={{0,16},{1,19},{4,20},{5,23},{8,24},{9,27},{12,28},{13,31},{32,48},... | collective-permute-start | bytes 663560 | tf_op jit(solution)/shard_map/ppermute | solution.py:37
  6.8 1.6 %collective-permute-start.3 = (bf16[144,768]{1,0:T(8,128)(2,1)S(1)}, bf16[144,768]{1,0:T(8,128)(2,1)S(1)}, u32[]{:S(2)}, u32[]{:S(2)}) collective-permute-start(bf16[144,768]{1,0:T(8,128)(2,1)S(1)} %get-tuple-element.31.refs_2_), channel_id=1, source_target_pairs={{0,32},{1,5},{4,36},{5,9},{8,40},{9,13},{12,44},{13,1},{32,64},{33... | collective-permute-start | bytes 663560 | tf_op jit(solution)/shard_map/ppermute | solution.py:37
  8.4 3.3 %collective-permute-start.2 = (bf16[144,768]{1,0:T(8,128)(2,1)S(1)}, bf16[144,768]{1,0:T(8,128)(2,1)S(1)}, u32[]{:S(2)}, u32[]{:S(2)}) collective-permute-start(bf16[144,768]{1,0:T(8,128)(2,1)S(1)} %get-tuple-element.31.refs_2_), channel_id=1, source_target_pairs={{0,64},{1,9},{4,68},{5,13},{8,72},{9,1},{12,76},{13,5},{32,96},{33... | collective-permute-start | bytes 663560 | tf_op jit(solution)/shard_map/ppermute | solution.py:37
  13.8 3.5 %collective-permute-done.2.refs_4_ = bf16[144,768]{1,0:T(8,128)(2,1)S(1)} collective-permute-done((bf16[144,768]{1,0:T(8,128)(2,1)S(1)}, bf16[144,768]{1,0:T(8,128)(2,1)S(1)}, u32[]{:S(2)}, u32[]{:S(2)}) %collective-permute-start.2) | collective-permute-done | bytes 221216 | tf_op jit(solution)/shard_map/ppermute | solution.py:37
  17.6 1.9 %collective-permute-start.8 = (bf16[272,768]{1,0:T(8,128)(2,1)S(1)}, bf16[272,768]{1,0:T(8,128)(2,1)S(1)}, u32[]{:S(2)}, u32[]{:S(2)}) collective-permute-start(bf16[272,768]{1,0:T(8,128)(2,1)S(1)} %get-tuple-element.33.refs_0_), channel_id=1, source_target_pairs={{0,1},{1,0},{4,5},{5,4},{8,9},{9,8},{12,13},{13,12},{32,33},{33,32... | collective-permute-start | bytes 1253384 | tf_op jit(solution)/shard_map/ppermute | solution.py:37
  20.8 1.8 %collective-permute-start.5 = (bf16[272,768]{1,0:T(8,128)(2,1)S(1)}, bf16[272,768]{1,0:T(8,128)(2,1)S(1)}, u32[]{:S(2)}, u32[]{:S(2)}) collective-permute-start(bf16[272,768]{1,0:T(8,128)(2,1)S(1)} %get-tuple-element.33.refs_0_), channel_id=1, source_target_pairs={{0,8},{1,65},{4,12},{5,69},{8,0},{9,73},{12,4},{13,77},{32,40},{33... | collective-permute-start | bytes 1253384 | tf_op jit(solution)/shard_map/ppermute | solution.py:37
  22.7 1.5 %collective-permute-start.4 = (bf16[272,768]{1,0:T(8,128)(2,1)S(1)}, bf16[272,768]{1,0:T(8,128)(2,1)S(1)}, u32[]{:S(2)}, u32[]{:S(2)}) collective-permute-start(bf16[272,768]{1,0:T(8,128)(2,1)S(1)} %get-tuple-element.33.refs_0_), channel_id=1, source_target_pairs={{0,12},{1,97},{4,0},{5,101},{8,4},{9,105},{12,8},{13,109},{32,44},... | collective-permute-start | bytes 1253384 | tf_op jit(solution)/shard_map/ppermute | solution.py:37
  24.1 1.9 %collective-permute-start.12 = (bf16[528,768]{1,0:T(8,128)(2,1)S(1)}, bf16[528,768]{1,0:T(8,128)(2,1)S(1)}, u32[]{:S(2)}, u32[]{:S(2)}) collective-permute-start(bf16[528,768]{1,0:T(8,128)(2,1)S(1)} %get-tuple-element.34.refs_4_), channel_id=1, source_target_pairs={{0,1},{1,0},{4,5},{5,4},{8,9},{9,8},{12,13},{13,12},{32,33},{33,32... | collective-permute-start | bytes 2433032 | tf_op jit(solution)/shard_map/ppermute | solution.py:37
  26.0 3.0 %collective-permute-done.7.refs_5_ = bf16[528,768]{1,0:T(8,128)(2,1)S(1)} collective-permute-done((bf16[528,768]{1,0:T(8,128)(2,1)S(1)}, bf16[528,768]{1,0:T(8,128)(2,1)S(1)}, u32[]{:S(2)}, u32[]{:S(2)}) %collective-permute-start.7) | collective-permute-done | bytes 811040 | tf_op jit(solution)/shard_map/ppermute | solution.py:37
  29.0 1.9 %collective-permute-start.13 = (bf16[528,768]{1,0:T(8,128)(2,1)S(1)}, bf16[528,768]{1,0:T(8,128)(2,1)S(1)}, u32[]{:S(2)}, u32[]{:S(2)}) collective-permute-start(bf16[528,768]{1,0:T(8,128)(2,1)S(1)} %collective-permute-done.7.refs_5_), channel_id=1, source_target_pairs={{0,1},{1,0},{4,5},{5,4},{8,9},{9,8},{12,13},{13,12},{32,33},{33,32... | collective-permute-start | bytes 2433032 | tf_op jit(solution)/shard_map/ppermute | solution.py:37
  30.8 2.0 %collective-permute-done.5.refs_2_ = bf16[272,768]{1,0:T(8,128)(2,1)S(1)} collective-permute-done((bf16[272,768]{1,0:T(8,128)(2,1)S(1)}, bf16[272,768]{1,0:T(8,128)(2,1)S(1)}, u32[]{:S(2)}, u32[]{:S(2)}) %collective-permute-start.5) | collective-permute-done | bytes 417824 | tf_op jit(solution)/shard_map/ppermute | solution.py:37
  32.9 2.6 %collective-permute-start.10 = (bf16[272,768]{1,0:T(8,128)(2,1)S(1)}, bf16[272,768]{1,0:T(8,128)(2,1)S(1)}, u32[]{:S(2)}, u32[]{:S(2)}) collective-permute-start(bf16[272,768]{1,0:T(8,128)(2,1)S(1)} %collective-permute-done.5.refs_2_), channel_id=1, source_target_pairs={{0,1},{1,0},{4,5},{5,4},{8,9},{9,8},{12,13},{13,12},{32,33},{33,32... | collective-permute-start | bytes 1253384 | tf_op jit(solution)/shard_map/ppermute | solution.py:37
  35.5 4.3 %shard_map.78 = (f32[1024,768]{1,0:T(8,128)S(1)}, bf16[2048,1024]{1,0:T(8,128)(2,1)S(1)}, bf16[2048,768]{1,0:T(8,128)(2,1)S(1)}, f32[3,8,128]{2,1,0:T(8,128)S(1)}, bf16[1024,768]{1,0:T(8,128)(2,1)S(1)}) custom-call(f32[8,128]{1,0:T(8,128)S(1)} %get-tuple-element.32.given, bf16[272,768]{1,0:T(8,128)(2,1)S(1)} %get-tuple-element.33.refs_0_, ...), custom_call_target="tpu_custom_call" | custom-call | flops 3221225472 | bytes 12582912 | tf_op jit(solution)/shard_map/pallas_call | solution.py:327
  39.9 2.6 %shard_map.79 = (f32[512,768]{1,0:T(8,128)S(1)}, bf16[2048,1024]{1,0:T(8,128)(2,1)S(1)}, bf16[2048,768]{1,0:T(8,128)(2,1)S(1)}, f32[3,8,128]{2,1,0:T(8,128)S(1)}) custom-call(f32[8,128]{1,0:T(8,128)S(1)} %get-tuple-element.32.given, bf16[272,768]{1,0:T(8,128)(2,1)S(1)} %collective-permute-done.8.refs_0_, ...), custom_call_target="tpu_custom_call", output_to_operand_aliasing={{1}: (7, {}), {2}: (8, {})} | custom-call | flops 1610612736 | bytes 6291456 | tf_op jit(solution)/shard_map/pallas_call | solution.py:327
  43.1 2.8 %shard_map.80 = (f32[512,768]{1,0:T(8,128)S(1)}, bf16[2048,1024]{1,0:T(8,128)(2,1)S(1)}, bf16[2048,768]{1,0:T(8,128)(2,1)S(1)}, f32[3,8,128]{2,1,0:T(8,128)S(1)}) custom-call(f32[8,128]{1,0:T(8,128)S(1)} %get-tuple-element.32.given, bf16[272,768]{1,0:T(8,128)(2,1)S(1)} %collective-permute-done.8.refs_0_, ...), custom_call_target="tpu_custom_call", output_to_operand_aliasing={{1}: (7, {}), {2}: (8, {})} | custom-call | flops 1610612736 | bytes 6291456 | tf_op jit(solution)/shard_map/pallas_call | solution.py:327
  46.0 4.0 %shard_map.81 = (f32[512,768]{1,0:T(8,128)S(1)}, f32[512,768]{1,0:T(8,128)S(1)}, f32[128,128]{1,0:T(8,128)}) custom-call(f32[3,8,128]{2,1,0:T(8,128)S(1)} %get-tuple-element.35.refs_0_, f32[3,8,128]{2,1,0:T(8,128)S(1)} %get-tuple-element.39.refs_1_, f32[3,8,128]{2,1,0:T(8,128)S(1)} %get-tuple-element.42.refs_2_, bf16[1,128]{1,0:T(2,128)(2,1)S(1)} %bitcast.13, ...), custom_call_target="tpu_custom_call" | custom-call | flops 3221225472 | bytes 9437184 | tf_op jit(solution)/shard_map/pallas_call | solution.py:327
  57.1 8.7 %all-to-all-start = ((f32[128,1,128]{2,1,0:T(1,128)}), f32[128,1,128]{2,1,0:T(1,128)S(1)}, u32[]{:S(2)}, u32[]{:S(2)}) async-start(f32[128,1,128]{2,1,0:T(1,128)} %bitcast.2), calls=%async_computation | async-start | bytes 131072 | tf_op jit(solution)/shard_map/all_to_all | solution.py:427
  66.3 1.5 %fusion.3 = f32[256,768]{1,0:T(8,128)S(1)} fusion(f32[256,768]{1,0:T(8,128)S(1)} %get-tuple-element.51, f32[512,768]{1,0:T(8,128)S(1)} %get-tuple-element.58, f16[256,768]{1,0:T(8,128)(2,1)} %collective-permute-done.19, f16[256,768]{1,0:T(8,128)(2,1)} %collective-permute-done.18, f16[256,768]{1,0:T(8,128)(2,1)} %collective-permute-done.17), kind=kLoop, calls=%fused_computation.5 | loop fusion | flops 1572864 | bytes 3538944 | tf_op jit(solution)/shard_map/add | solution.py:426
  67.8 2.6 %collective-permute-start.20 = (f16[128,768]{1,0:T(8,128)(2,1)S(1)}, f16[128,768]{1,0:T(8,128)(2,1)S(1)}, u32[]{:S(2)}, u32[]{:S(2)}) collective-permute-start(f16[128,768]{1,0:T(8,128)(2,1)S(1)} %slice_convert_fusion), channel_id=1, source_target_pairs={{0,16},{1,19},{4,20},{5,23},{8,24},{9,27},{12,28},{13,31},{32,48},... | collective-permute-start | bytes 589832 | tf_op jit(solution)/shard_map/ppermute | solution.py:37
  70.5 1.4 %collective-permute-start.21 = (f16[128,768]{1,0:T(8,128)(2,1)S(1)}, f16[128,768]{1,0:T(8,128)(2,1)S(1)}, u32[]{:S(2)}, u32[]{:S(2)}) collective-permute-start(f16[128,768]{1,0:T(8,128)(2,1)S(1)} %get-tuple-element.62), channel_id=1, source_target_pairs={{0,32},{1,5},{4,36},{5,9},{8,40},{9,13},{12,44},{13,1},{32,64},{33... | collective-permute-start | bytes 589832 | tf_op jit(solution)/shard_map/ppermute | solution.py:37
  71.9 1.8 %collective-permute-start.23 = (f16[128,768]{1,0:T(8,128)(2,1)S(1)}, f16[128,768]{1,0:T(8,128)(2,1)S(1)}, u32[]{:S(2)}, u32[]{:S(2)}) collective-permute-start(f16[128,768]{1,0:T(8,128)(2,1)S(1)} %get-tuple-element.63), channel_id=1, source_target_pairs={{0,96},{1,13},{4,100},{5,1},{8,104},{9,5},{12,108},{13,9},{32,0},{... | collective-permute-start | bytes 589832 | tf_op jit(solution)/shard_map/ppermute | solution.py:37
  75.2 1.6 %collective-permute-done.21 = f16[128,768]{1,0:T(8,128)(2,1)S(1)} collective-permute-done((f16[128,768]{1,0:T(8,128)(2,1)S(1)}, f16[128,768]{1,0:T(8,128)(2,1)S(1)}, u32[]{:S(2)}, u32[]{:S(2)}) %collective-permute-start.21) | collective-permute-done | bytes 196640 | tf_op jit(solution)/shard_map/ppermute | solution.py:37
  76.8 1.6 %collective-permute-done.23 = f16[128,768]{1,0:T(8,128)(2,1)S(1)} collective-permute-done((f16[128,768]{1,0:T(8,128)(2,1)S(1)}, f16[128,768]{1,0:T(8,128)(2,1)S(1)}, u32[]{:S(2)}, u32[]{:S(2)}) %collective-permute-start.23) | collective-permute-done | bytes 196640 | tf_op jit(solution)/shard_map/ppermute | solution.py:37
  78.4 1.5 %collective-permute-done.22 = f16[128,768]{1,0:T(8,128)(2,1)S(1)} collective-permute-done((f16[128,768]{1,0:T(8,128)(2,1)S(1)}, f16[128,768]{1,0:T(8,128)(2,1)S(1)}, u32[]{:S(2)}, u32[]{:S(2)}) %collective-permute-start.22) | collective-permute-done | bytes 196640 | tf_op jit(solution)/shard_map/ppermute | solution.py:37
  (56 shorter events, 16.6 us)
Async XLA Ops:
  3.4 10.4 %collective-permute-start = (bf16[144,768]{1,0:T(8,128)(2,1)S(1)}, bf16[144,768]{1,0:T(8,128)(2,1)S(1)}, u32[]{:S(2)}, u32[]{:S(2)}) collective-permute-start(bf16[144,768]{1,0:T(8,128)(2,1)S(1)} %get-tuple-element.30.refs_0_), channel_id=1, source_target_pairs={{0,16},{1,19},{4,20},{5,23},{8,24},{9,27},{12,28},{13,31},{32,48},... | collective-permute-start | bytes 663560 | tf_op jit(solution)/shard_map/ppermute | solution.py:37
  6.8 7.1 %collective-permute-start.3 = (bf16[144,768]{1,0:T(8,128)(2,1)S(1)}, bf16[144,768]{1,0:T(8,128)(2,1)S(1)}, u32[]{:S(2)}, u32[]{:S(2)}) collective-permute-start(bf16[144,768]{1,0:T(8,128)(2,1)S(1)} %get-tuple-element.31.refs_2_), channel_id=1, source_target_pairs={{0,32},{1,5},{4,36},{5,9},{8,40},{9,13},{12,44},{13,1},{32,64},{33... | collective-permute-start | bytes 663560 | tf_op jit(solution)/shard_map/ppermute | solution.py:37
  8.4 9.0 %collective-permute-start.2 = (bf16[144,768]{1,0:T(8,128)(2,1)S(1)}, bf16[144,768]{1,0:T(8,128)(2,1)S(1)}, u32[]{:S(2)}, u32[]{:S(2)}) collective-permute-start(bf16[144,768]{1,0:T(8,128)(2,1)S(1)} %get-tuple-element.31.refs_2_), channel_id=1, source_target_pairs={{0,64},{1,9},{4,68},{5,13},{8,72},{9,1},{12,76},{13,5},{32,96},{33... | collective-permute-start | bytes 663560 | tf_op jit(solution)/shard_map/ppermute | solution.py:37
  11.7 5.7 %collective-permute-start.1 = (bf16[144,768]{1,0:T(8,128)(2,1)S(1)}, bf16[144,768]{1,0:T(8,128)(2,1)S(1)}, u32[]{:S(2)}, u32[]{:S(2)}) collective-permute-start(bf16[144,768]{1,0:T(8,128)(2,1)S(1)} %get-tuple-element.31.refs_2_), channel_id=1, source_target_pairs={{0,96},{1,13},{4,100},{5,1},{8,104},{9,5},{12,108},{13,9},{32,0},{... | collective-permute-start | bytes 663560 | tf_op jit(solution)/shard_map/ppermute | solution.py:37
  17.5 11.5 %collective-permute-start.7 = (bf16[528,768]{1,0:T(8,128)(2,1)S(1)}, bf16[528,768]{1,0:T(8,128)(2,1)S(1)}, u32[]{:S(2)}, u32[]{:S(2)}) collective-permute-start(bf16[528,768]{1,0:T(8,128)(2,1)S(1)} %get-tuple-element.34.refs_4_), channel_id=1, source_target_pairs={{0,18},{1,17},{4,22},{5,21},{8,26},{9,25},{12,30},{13,29},{32,50},... | collective-permute-start | bytes 2433032 | tf_op jit(solution)/shard_map/ppermute | solution.py:37
  17.6 6.5 %collective-permute-start.8 = (bf16[272,768]{1,0:T(8,128)(2,1)S(1)}, bf16[272,768]{1,0:T(8,128)(2,1)S(1)}, u32[]{:S(2)}, u32[]{:S(2)}) collective-permute-start(bf16[272,768]{1,0:T(8,128)(2,1)S(1)} %get-tuple-element.33.refs_0_), channel_id=1, source_target_pairs={{0,1},{1,0},{4,5},{5,4},{8,9},{9,8},{12,13},{13,12},{32,33},{33,32... | collective-permute-start | bytes 1253384 | tf_op jit(solution)/shard_map/ppermute | solution.py:37
  19.5 11.4 %collective-permute-start.6 = (bf16[272,768]{1,0:T(8,128)(2,1)S(1)}, bf16[272,768]{1,0:T(8,128)(2,1)S(1)}, u32[]{:S(2)}, u32[]{:S(2)}) collective-permute-start(bf16[272,768]{1,0:T(8,128)(2,1)S(1)} %get-tuple-element.33.refs_0_), channel_id=1, source_target_pairs={{0,4},{1,33},{4,8},{5,37},{8,12},{9,41},{12,0},{13,45},{32,36},{33... | collective-permute-start | bytes 1253384 | tf_op jit(solution)/shard_map/ppermute | solution.py:37
  20.8 12.0 %collective-permute-start.5 = (bf16[272,768]{1,0:T(8,128)(2,1)S(1)}, bf16[272,768]{1,0:T(8,128)(2,1)S(1)}, u32[]{:S(2)}, u32[]{:S(2)}) collective-permute-start(bf16[272,768]{1,0:T(8,128)(2,1)S(1)} %get-tuple-element.33.refs_0_), channel_id=1, source_target_pairs={{0,8},{1,65},{4,12},{5,69},{8,0},{9,73},{12,4},{13,77},{32,40},{33... | collective-permute-start | bytes 1253384 | tf_op jit(solution)/shard_map/ppermute | solution.py:37
  22.7 12.8 %collective-permute-start.4 = (bf16[272,768]{1,0:T(8,128)(2,1)S(1)}, bf16[272,768]{1,0:T(8,128)(2,1)S(1)}, u32[]{:S(2)}, u32[]{:S(2)}) collective-permute-start(bf16[272,768]{1,0:T(8,128)(2,1)S(1)} %get-tuple-element.33.refs_0_), channel_id=1, source_target_pairs={{0,12},{1,97},{4,0},{5,101},{8,4},{9,105},{12,8},{13,109},{32,44},... | collective-permute-start | bytes 1253384 | tf_op jit(solution)/shard_map/ppermute | solution.py:37
  24.1 15.7 %collective-permute-start.12 = (bf16[528,768]{1,0:T(8,128)(2,1)S(1)}, bf16[528,768]{1,0:T(8,128)(2,1)S(1)}, u32[]{:S(2)}, u32[]{:S(2)}) collective-permute-start(bf16[528,768]{1,0:T(8,128)(2,1)S(1)} %get-tuple-element.34.refs_4_), channel_id=1, source_target_pairs={{0,1},{1,0},{4,5},{5,4},{8,9},{9,8},{12,13},{13,12},{32,33},{33,32... | collective-permute-start | bytes 2433032 | tf_op jit(solution)/shard_map/ppermute | solution.py:37
  29.0 14.1 %collective-permute-start.13 = (bf16[528,768]{1,0:T(8,128)(2,1)S(1)}, bf16[528,768]{1,0:T(8,128)(2,1)S(1)}, u32[]{:S(2)}, u32[]{:S(2)}) collective-permute-start(bf16[528,768]{1,0:T(8,128)(2,1)S(1)} %collective-permute-done.7.refs_5_), channel_id=1, source_target_pairs={{0,1},{1,0},{4,5},{5,4},{8,9},{9,8},{12,13},{13,12},{32,33},{33,32... | collective-permute-start | bytes 2433032 | tf_op jit(solution)/shard_map/ppermute | solution.py:37
  30.8 9.0 %collective-permute-start.11 = (bf16[272,768]{1,0:T(8,128)(2,1)S(1)}, bf16[272,768]{1,0:T(8,128)(2,1)S(1)}, u32[]{:S(2)}, u32[]{:S(2)}) collective-permute-start(bf16[272,768]{1,0:T(8,128)(2,1)S(1)} %collective-permute-done.6.refs_3_), channel_id=1, source_target_pairs={{0,1},{1,0},{4,5},{5,4},{8,9},{9,8},{12,13},{13,12},{32,33},{33,32... | collective-permute-start | bytes 1253384 | tf_op jit(solution)/shard_map/ppermute | solution.py:37
  32.9 7.0 %collective-permute-start.10 = (bf16[272,768]{1,0:T(8,128)(2,1)S(1)}, bf16[272,768]{1,0:T(8,128)(2,1)S(1)}, u32[]{:S(2)}, u32[]{:S(2)}) collective-permute-start(bf16[272,768]{1,0:T(8,128)(2,1)S(1)} %collective-permute-done.5.refs_2_), channel_id=1, source_target_pairs={{0,1},{1,0},{4,5},{5,4},{8,9},{9,8},{12,13},{13,12},{32,33},{33,32... | collective-permute-start | bytes 1253384 | tf_op jit(solution)/shard_map/ppermute | solution.py:37
  35.5 4.4 %collective-permute-start.9 = (bf16[272,768]{1,0:T(8,128)(2,1)S(1)}, bf16[272,768]{1,0:T(8,128)(2,1)S(1)}, u32[]{:S(2)}, u32[]{:S(2)}) collective-permute-start(bf16[272,768]{1,0:T(8,128)(2,1)S(1)} %collective-permute-done.4.refs_1_), channel_id=1, source_target_pairs={{0,1},{1,0},{4,5},{5,4},{8,9},{9,8},{12,13},{13,12},{32,33},{33,32... | collective-permute-start | bytes 1253384 | tf_op jit(solution)/shard_map/ppermute | solution.py:37
  42.5 7.5 %collective-permute-start.14 = (f32[512,768]{1,0:T(8,128)S(1)}, f32[512,768]{1,0:T(8,128)S(1)}, u32[]{:S(2)}, u32[]{:S(2)}) collective-permute-start(f32[512,768]{1,0:T(8,128)S(1)} %get-tuple-element.47), channel_id=1, source_target_pairs={{0,1},{1,0},{4,5},{5,4},{8,9},{9,8},{12,13},{13,12},{32,33},{33,32... | collective-permute-start | bytes 4718600 | tf_op jit(solution)/shard_map/ppermute | solution.py:37
  51.6 14.3 %collective-permute-start.16 = (f16[512,768]{1,0:T(8,128)(2,1)}, f16[512,768]{1,0:T(8,128)(2,1)S(1)}, u32[]{:S(2)}, u32[]{:S(2)}) collective-permute-start(f16[512,768]{1,0:T(8,128)(2,1)} %convert_element_type.43), channel_id=1, source_target_pairs={{0,18},{1,17},{4,22},{5,21},{8,26},{9,25},{12,30},{13,29},{32,50},... | collective-permute-start | bytes 2359304 | tf_op jit(solution)/shard_map/ppermute | solution.py:37
  53.1 13.0 %collective-permute-start.17 = (f16[256,768]{1,0:T(8,128)(2,1)}, f16[256,768]{1,0:T(8,128)(2,1)}, u32[]{:S(2)}, u32[]{:S(2)}) collective-permute-start(f16[256,768]{1,0:T(8,128)(2,1)} %get-tuple-element.59), channel_id=1, source_target_pairs={{0,4},{1,33},{4,8},{5,37},{8,12},{9,41},{12,0},{13,45},{32,36},{33... | collective-permute-start | bytes 1179656 | tf_op jit(solution)/shard_map/ppermute | solution.py:37
  54.5 11.7 %collective-permute-start.19 = (f16[256,768]{1,0:T(8,128)(2,1)}, f16[256,768]{1,0:T(8,128)(2,1)}, u32[]{:S(2)}, u32[]{:S(2)}) collective-permute-start(f16[256,768]{1,0:T(8,128)(2,1)} %get-tuple-element.60), channel_id=1, source_target_pairs={{0,12},{1,97},{4,0},{5,101},{8,4},{9,105},{12,8},{13,109},{32,44},... | collective-permute-start | bytes 1179656 | tf_op jit(solution)/shard_map/ppermute | solution.py:37
  55.8 10.5 %collective-permute-start.18 = (f16[256,768]{1,0:T(8,128)(2,1)}, f16[256,768]{1,0:T(8,128)(2,1)}, u32[]{:S(2)}, u32[]{:S(2)}) collective-permute-start(f16[256,768]{1,0:T(8,128)(2,1)} %get-tuple-element.61), channel_id=1, source_target_pairs={{0,8},{1,65},{4,12},{5,69},{8,0},{9,73},{12,4},{13,77},{32,40},{33... | collective-permute-start | bytes 1179656 | tf_op jit(solution)/shard_map/ppermute | solution.py:37
  57.1 23.4 %all-to-all-start = ((f32[128,1,128]{2,1,0:T(1,128)}), f32[128,1,128]{2,1,0:T(1,128)S(1)}, u32[]{:S(2)}, u32[]{:S(2)}) async-start(f32[128,1,128]{2,1,0:T(1,128)} %bitcast.2), calls=%async_computation | async-start | bytes 131072 | tf_op jit(solution)/shard_map/all_to_all | solution.py:427
  67.8 7.3 %collective-permute-start.20 = (f16[128,768]{1,0:T(8,128)(2,1)S(1)}, f16[128,768]{1,0:T(8,128)(2,1)S(1)}, u32[]{:S(2)}, u32[]{:S(2)}) collective-permute-start(f16[128,768]{1,0:T(8,128)(2,1)S(1)} %slice_convert_fusion), channel_id=1, source_target_pairs={{0,16},{1,19},{4,20},{5,23},{8,24},{9,27},{12,28},{13,31},{32,48},... | collective-permute-start | bytes 589832 | tf_op jit(solution)/shard_map/ppermute | solution.py:37
  70.5 6.3 %collective-permute-start.21 = (f16[128,768]{1,0:T(8,128)(2,1)S(1)}, f16[128,768]{1,0:T(8,128)(2,1)S(1)}, u32[]{:S(2)}, u32[]{:S(2)}) collective-permute-start(f16[128,768]{1,0:T(8,128)(2,1)S(1)} %get-tuple-element.62), channel_id=1, source_target_pairs={{0,32},{1,5},{4,36},{5,9},{8,40},{9,13},{12,44},{13,1},{32,64},{33... | collective-permute-start | bytes 589832 | tf_op jit(solution)/shard_map/ppermute | solution.py:37
  71.9 6.6 %collective-permute-start.23 = (f16[128,768]{1,0:T(8,128)(2,1)S(1)}, f16[128,768]{1,0:T(8,128)(2,1)S(1)}, u32[]{:S(2)}, u32[]{:S(2)}) collective-permute-start(f16[128,768]{1,0:T(8,128)(2,1)S(1)} %get-tuple-element.63), channel_id=1, source_target_pairs={{0,96},{1,13},{4,100},{5,1},{8,104},{9,5},{12,108},{13,9},{32,0},{... | collective-permute-start | bytes 589832 | tf_op jit(solution)/shard_map/ppermute | solution.py:37
  73.7 6.3 %collective-permute-start.22 = (f16[128,768]{1,0:T(8,128)(2,1)S(1)}, f16[128,768]{1,0:T(8,128)(2,1)S(1)}, u32[]{:S(2)}, u32[]{:S(2)}) collective-permute-start(f16[128,768]{1,0:T(8,128)(2,1)S(1)} %get-tuple-element.64), channel_id=1, source_target_pairs={{0,64},{1,9},{4,68},{5,13},{8,72},{9,1},{12,76},{13,5},{32,96},{33... | collective-permute-start | bytes 589832 | tf_op jit(solution)/shard_map/ppermute | solution.py:37
  (7 other events, 29.0 us)
